TPU v7x, 32 devices: a whole 2x2x4 slice. The times are simulated.
32 devices in a mesh: grp: 2 (over y), node: 4 (over z), sub: 2 (over x), rep: 2 (over core).
Axes of the slice: x: 2, y: 2, z: 4, core: 2. Of those that a mesh axis runs over, the one named last changes fastest.
Arguments:
- meson_nodes: float32 [2, 16, 512, 512], P(None, ('grp', 'node'), 'sub', 'rep'), parts along dimension 1, may hold values from -0.66 to 0.66
- term_nodes: int32 [8, 2], P('grp'), parts along dimension 0, may hold values from 0 to 7, as said below
- weight_codes: int32 [8], P('grp'), parts along dimension 0, may hold values from 0 to 7
- resident_pick: int32 [16], P('grp'), parts along dimension 0, may hold values from 0 to 1
Outputs:
- contracted: float32 [2, 16, 512, 512], P(None, ('grp', 'node'), 'sub', 'rep'), parts along dimension 1
There are 2 independent parts, one for each index of `grp`. A program takes and returns all parts, laid end to end along the dimension named above; each array names one. Nothing has to cross between parts.
Inputs may be any that keep to these rules, and one draw needn't show every extreme that they name: `term_nodes`: node n belongs to owner n // 2. In every term the two nodes differ. The first nodes of at most 2 terms belong to any one owner, and those of exactly 2 terms to some owner.
All inputs are finite; a program needn't handle non-finite values.
Results may differ from a plain program's by a relative error of at most 0.000098.
Values sent between devices are 32-bit elements; how exact they have to be, the bound alone decides.
No kernel may reach another device: no remote copies, remote signals or barrier semaphores. Data moves between devices by JAX's collectives and lax.ppermute only.
A program may use at most 64 MiB of HBM per device.

v0:
```python
import jax
import jax.numpy as jnp
from jax import lax
from jax.sharding import PartitionSpec as P


def complex_step(full_left, segment):
    highest = lax.Precision.HIGHEST
    real_part = jnp.einsum(
        "kij,kjl->kil",
        full_left[0],
        segment[0],
        precision=highest,
        preferred_element_type=jnp.float32,
    ) - jnp.einsum(
        "kij,kjl->kil",
        full_left[1],
        segment[1],
        precision=highest,
        preferred_element_type=jnp.float32,
    )
    imag_part = jnp.einsum(
        "kij,kjl->kil",
        full_left[0],
        segment[1],
        precision=highest,
        preferred_element_type=jnp.float32,
    ) + jnp.einsum(
        "kij,kjl->kil",
        full_left[1],
        segment[0],
        precision=highest,
        preferred_element_type=jnp.float32,
    )
    return jnp.stack([real_part, imag_part])


def body(meson_nodes, term_nodes, weight_codes, resident_pick):
    node_count = lax.axis_size("node")
    owned = meson_nodes.shape[1]
    row_count = meson_nodes.shape[2]
    col_count = meson_nodes.shape[3]
    band = row_count // node_count
    total_nodes = owned * node_count
    term_count = term_nodes.shape[0]
    banded = meson_nodes.reshape(2, owned, node_count, band * col_count)
    spread = lax.all_to_all(banded, "node", split_axis=2, concat_axis=1, tiled=True).reshape(
        2, total_nodes, band * col_count
    )
    leading = term_nodes[:, 0]
    trailing = term_nodes[:, 1]
    worker_ids = jnp.arange(node_count, dtype=jnp.int32)
    slot_count = term_count // node_count
    table = jnp.arange(slot_count, dtype=jnp.int32)[None, :] * node_count + worker_ids[:, None]
    active = jnp.ones(table.shape, jnp.float32)
    first_table = leading[table]
    second_table = trailing[table]
    factors = active * (weight_codes[table].astype(jnp.float32) - 3.5) * 0.5
    wanted = jnp.stack([first_table.T, second_table.T], axis=1)
    picked = jnp.take(spread, wanted, axis=1)
    fetched = lax.all_to_all(picked, "node", split_axis=3, concat_axis=3, tiled=True).reshape(
        2, slot_count, 2, row_count, col_count
    )
    left_rows = fetched[:, :, 0]
    right_band = fetched[:, :, 1]
    left_full = lax.all_gather(left_rows, "rep", axis=3, tiled=True)
    products = complex_step(left_full, lax.all_gather(right_band, "sub", axis=2, tiled=True))
    outgoing = products.reshape(2, slot_count, node_count, band * col_count)
    returned = lax.all_to_all(outgoing, "node", split_axis=2, concat_axis=1, tiled=True).reshape(
        2, node_count * slot_count, band * col_count
    )
    node_ids = jnp.arange(total_nodes, dtype=jnp.int32)
    incidence = (first_table.reshape(-1)[:, None] == node_ids[None, :]).astype(jnp.float32) + (
        second_table.reshape(-1)[:, None] == node_ids[None, :]
    ).astype(jnp.float32)
    mixing = factors.reshape(-1)[:, None] * incidence
    summed = jnp.einsum("mn,cmx->cnx", mixing, returned, precision=lax.Precision.HIGHEST)
    owner_sum = lax.all_to_all(
        summed.reshape(2, total_nodes, 1, band * col_count),
        "node",
        split_axis=1,
        concat_axis=2,
        tiled=True,
    ).reshape(2, owned, row_count, col_count)
    sum_full = lax.all_gather(owner_sum, "rep", axis=3, tiled=True)
    own_index = lax.axis_index("node")
    picks = lax.dynamic_slice_in_dim(resident_pick, own_index * owned, owned)
    resident = jnp.take(meson_nodes, picks, axis=1)
    return complex_step(sum_full, lax.all_gather(resident, "sub", axis=2, tiled=True))


def solution(mesh):
    in_specs = (P(None, ("grp", "node"), "sub", "rep"), P("grp", None), P("grp"), P("grp"))
    out_specs = P(None, ("grp", "node"), "sub", "rep")
    return jax.shard_map(body, mesh=mesh, in_specs=in_specs, out_specs=out_specs, check_vma=False)
```

profile of v0, /device:TPU:0, one launch (start us, length us, event | category | flops | bytes accessed | tf_op | source)
XLA Modules:
  0.0 191.7 jit_solution(10941233466209382767)
XLA Ops:
  6.5 1.8 reshape.311
  8.3 1.8 copy.20
  10.1 6.3 %all-to-all-start = ((f32[2,2,4,16384]{3,0,1,2:T(2,128)}), f32[2,2,4,16384]{3,0,1,2:T(2,128)S(1)}, u32[]{:S(2)}, u32[]{:S(2)}) async-start(f32[2,2,4,16384]{3,0,1,2:T(2,128)} %copy.20), calls=%async_computation | async-start | bytes 2097152 | tf_op jit(solution)/shard_map/all_to_all | solution.py:47
  18.0 24.2 %all-to-all-done = f32[2,2,4,16384]{3,0,1,2:T(2,128)S(1)} async-done(((f32[2,2,4,16384]{3,0,1,2:T(2,128)}), f32[2,2,4,16384]{3,0,1,2:T(2,128)S(1)}, u32[]{:S(2)}, u32[]{:S(2)}) %all-to-all-start) | async-done | bytes 1048608 | tf_op jit(solution)/shard_map/all_to_all | solution.py:47
  42.1 1.7 gather_fusion.2
  44.9 27.7 %all_to_all.44 = f32[2,1,2,4,16384]{4,2,0,1,3:T(2,128)S(1)} all-to-all(f32[2,1,2,4,16384]{4,2,0,1,3:T(2,128)S(1)} %bitcast_select_fusion), channel_id=1, replica_groups=mesh['grp'=2,'node'=4,'sub'=2,'rep'=2] {'node'}, dimensions={3} | all-to-all | bytes 2097152 | tf_op jit(solution)/shard_map/all_to_all | solution.py:61
  75.9 19.8 %all-gather.13.cloned.1.call-done = f32[2,1,1,512,256]{4,3,2,0,1:T(8,128)} async-done(((f32[2,1,1,256,256]{4,3,2,0,1:T(8,128)}), f32[2,1,1,512,256]{4,3,2,0,1:T(8,128)}) %all-gather.13.cloned.1.call-update) | async-done | bytes 1048592 | tf_op jit(solution)/shard_map/all_gather | solution.py:67
  95.6 10.6 %all-gather.11.cloned.1.call-done = f32[2,1,1,256,512]{4,3,2,0,1:T(8,128)} async-done(((f32[2,1,1,256,256]{4,3,2,0,1:T(8,128)}), f32[2,1,1,256,512]{4,3,2,0,1:T(8,128)}) %all-gather.11.cloned.1.call-update) | async-done | bytes 1048592 | tf_op jit(solution)/shard_map/all_gather | solution.py:66
  106.2 1.9 fusion.7
  108.1 1.8 convolution_add_fusion.1
  110.9 1.3 convolution_subtract_fusion.1
  112.2 1.2 stack.43
  113.4 1.3 pad_maximum_fusion.1
  114.7 4.9 %all-to-all-start.2 = ((f32[2,1,4,16384]{3,0,1,2:T(2,128)}), f32[2,1,4,16384]{3,0,1,2:T(2,128)S(1)}, u32[]{:S(2)}, u32[]{:S(2)}) async-start(f32[2,1,4,16384]{3,0,1,2:T(2,128)} %pad_maximum_fusion.1), calls=%async_computation.2 | async-start | bytes 1048576 | tf_op jit(solution)/shard_map/all_to_all | solution.py:69
  120.2 1.2 fusion.2
  122.3 12.1 %all-to-all-done.2 = f32[2,1,4,16384]{3,0,1,2:T(2,128)S(1)} async-done(((f32[2,1,4,16384]{3,0,1,2:T(2,128)}), f32[2,1,4,16384]{3,0,1,2:T(2,128)S(1)}, u32[]{:S(2)}, u32[]{:S(2)}) %all-to-all-start.2) | async-done | bytes 524320 | tf_op jit(solution)/shard_map/all_to_all | solution.py:69
  134.5 1.4 convolution_bitcast_fusion
  136.7 27.8 %all_to_all.45 = f32[2,8,1,16384]{3,0,2,1:T(2,128)S(1)} all-to-all(f32[2,8,1,16384]{3,0,2,1:T(2,128)S(1)} %copy.26), channel_id=1, replica_groups=mesh['grp'=2,'node'=4,'sub'=2,'rep'=2] {'node'}, dimensions={1} | all-to-all | bytes 2097152 | tf_op jit(solution)/shard_map/all_to_all | solution.py:78
  165.1 1.7 reshape.320
  166.9 9.7 %all-gather.7.cloned.1.call-done = f32[2,2,256,512]{3,2,1,0:T(8,128)} async-done(((f32[2,2,256,256]{3,2,1,0:T(8,128)}), f32[2,2,256,512]{3,2,1,0:T(8,128)}) %all-gather.7.cloned.1.call-update) | async-done | bytes 2097168 | tf_op jit(solution)/shard_map/all_gather | solution.py:85
  176.6 2.8 %fusion.3 = f32[2,256,256]{2,1,0:T(8,128)S(1)} fusion(f32[2,2,256,512]{3,2,1,0:T(8,128)} %all-gather.7.cloned.1.call-done, f32[2,2,512,256]{3,2,1,0:T(8,128)} %all-gather.9.cloned.1.call-done), kind=kOutput, calls=%fused_computation.21 | convolution fusion | flops 805306368 | bytes 2621440 | tf_op jit(solution)/shard_map/kij,kjl->kil/dot_general | solution.py:22
  179.5 2.4 %fusion.4 = f32[2,256,256]{2,1,0:T(8,128)S(1)} fusion(f32[2,2,256,512]{3,2,1,0:T(8,128)} %all-gather.7.cloned.1.call-done, f32[2,2,512,256]{3,2,1,0:T(8,128)S(1)} %copy-done.1), kind=kOutput, calls=%fused_computation.22 | convolution fusion | flops 805306368 | bytes 2621440 | tf_op jit(solution)/shard_map/kij,kjl->kil/dot_general | solution.py:9
  181.8 1.1 fusion
  183.0 1.1 fusion.1
  (49 shorter events, 10.9 us)
Async XLA Ops:
  6.5 115.1 %copy-start = (s32[4]{0:T(128)S(1)}, s32[4]{0:T(128)}, u32[]{:S(2)}) copy-start(s32[4]{0:T(128)} %param.6) | copy-start | bytes 52
  8.3 8.1 %copy-start.6 = (s32[4,2]{0,1:T(2,128)S(1)}, s32[4,2]{0,1:T(2,128)}, u32[]{:S(2)}) copy-start(s32[4,2]{0,1:T(2,128)} %param.5) | copy-start | bytes 100
  10.1 32.0 %all-to-all-start = ((f32[2,2,4,16384]{3,0,1,2:T(2,128)}), f32[2,2,4,16384]{3,0,1,2:T(2,128)S(1)}, u32[]{:S(2)}, u32[]{:S(2)}) async-start(f32[2,2,4,16384]{3,0,1,2:T(2,128)} %copy.20), calls=%async_computation | async-start | bytes 2097152 | tf_op jit(solution)/shard_map/all_to_all | solution.py:47
  16.4 79.2 %all-gather.13.cloned.1.call-start = ((), (), s32[]{:S(2)}) async-start(), calls=%async_computation.7 | async-start | bytes 1572864 | tf_op jit(solution)/shard_map/all_gather | solution.py:67
  75.1 31.1 %all-gather.11.cloned.1.call-start = ((), (), s32[]{:S(2)}) async-start(), calls=%async_computation.6 | async-start | bytes 1572864 | tf_op jit(solution)/shard_map/all_gather | solution.py:66
  95.6 14.6 %copy-start.3 = (f32[2,1,1,512,256]{4,3,2,0,1:T(8,128)S(1)}, f32[2,1,1,512,256]{4,3,2,0,1:T(8,128)}, u32[]{:S(2)}) copy-start(f32[2,1,1,512,256]{4,3,2,0,1:T(8,128)} %all-gather.13.cloned.1.call-done) | copy-start | bytes 3145732
  106.2 4.0 %copy-start.4 = (f32[2,1,1,256,512]{4,3,2,0,1:T(8,128)S(1)}, f32[2,1,1,256,512]{4,3,2,0,1:T(8,128)}, u32[]{:S(2)}) copy-start(f32[2,1,1,256,512]{4,3,2,0,1:T(8,128)} %all-gather.11.cloned.1.call-done) | copy-start | bytes 3145732
  110.8 8.7 %copy-start.7 = (s32[8]{0:T(128)S(1)}, s32[8]{0:T(128)}, u32[]{:S(2)}) copy-start(s32[8]{0:T(128)} %param.7) | copy-start | bytes 100
  110.8 8.8 %copy-start.5 = (f32[2,2,256,256]{3,2,1,0:T(8,128)S(1)}, f32[2,2,256,256]{3,2,1,0:T(8,128)}, u32[]{:S(2)}) copy-start(f32[2,2,256,256]{3,2,1,0:T(8,128)} %param.4) | copy-start | bytes 3145732
  114.7 19.8 %all-to-all-start.2 = ((f32[2,1,4,16384]{3,0,1,2:T(2,128)}), f32[2,1,4,16384]{3,0,1,2:T(2,128)S(1)}, u32[]{:S(2)}, u32[]{:S(2)}) async-start(f32[2,1,4,16384]{3,0,1,2:T(2,128)} %pad_maximum_fusion.1), calls=%async_computation.2 | async-start | bytes 1048576 | tf_op jit(solution)/shard_map/all_to_all | solution.py:69
  119.5 47.4 %all-gather.9.cloned.1.call-start = ((), (), s32[]{:S(2)}) async-start(), calls=%async_computation.5 | async-start | bytes 3145728 | tf_op jit(solution)/shard_map/all_gather | solution.py:89
  121.4 55.2 %all-gather.7.cloned.1.call-start = ((), (), s32[]{:S(2)}) async-start(), calls=%async_computation.4 | async-start | bytes 3145728 | tf_op jit(solution)/shard_map/all_gather | solution.py:85
  166.9 12.6 %copy-start.1 = (f32[2,2,512,256]{3,2,1,0:T(8,128)S(1)}, f32[2,2,512,256]{3,2,1,0:T(8,128)}, u32[]{:S(2)}) copy-start(f32[2,2,512,256]{3,2,1,0:T(8,128)} %all-gather.9.cloned.1.call-done) | copy-start | bytes 6291460
  176.6 5.2 %copy-start.2 = (f32[2,2,256,512]{3,2,1,0:T(8,128)S(1)}, f32[2,2,256,512]{3,2,1,0:T(8,128)}, u32[]{:S(2)}) copy-start(f32[2,2,256,512]{3,2,1,0:T(8,128)} %all-gather.7.cloned.1.call-done) | copy-start | bytes 6291460
Sparse Core Ops, SparseCore 0:
  75.2 20.3 all-gather.12
  97.2 9.0 all-gather.10
  121.9 34.5 all-gather.8
  167.0 9.6 all-gather.6
where the time goes:
time: 192 us
  waiting for transfers between devices  77.2 us (40%)
  blocking collectives  55.5 us (29%)
  local copies, waits for them, and re-layouts  15.1 us (8%)
  matrix products  14.4 us (8%)
  between operations  13.4 us (7%)
  starting transfers between devices  11.4 us (6%)
  other arithmetic  4.75 us (2%)
    all_to_all x1, blocking collectives, body(): lax.all_to_all(summed.reshape(2, total_nodes, 1, band * col_count), 'node...  27.8 us
    all_to_all x1, blocking collectives, body(): lax.all_to_all(picked, 'node', split_axis=3, concat_axis=3, tiled=True)  27.7 us
    all_to_all x1, waiting for transfers between devices, body(): lax.all_to_all(banded, 'node', split_axis=2, concat_axis=1, tiled=True)  24.2 us
    all_gather x1, waiting for transfers between devices, body(): lax.all_gather(right_band, 'sub', axis=2, tiled=True)  19.8 us
    all_to_all x1, waiting for transfers between devices, body(): lax.all_to_all(outgoing, 'node', split_axis=2, concat_axis=1, tiled=True)  12.1 us
    all_gather x1, waiting for transfers between devices, body(): left_full = lax.all_gather(left_rows, 'rep', axis=3, tiled=True)  10.6 us
    all_gather x1, waiting for transfers between devices, body(): sum_full = lax.all_gather(owner_sum, 'rep', axis=3, tiled=True)  9.73 us
    all_to_all x1, starting transfers between devices, body(): lax.all_to_all(banded, 'node', split_axis=2, concat_axis=1, tiled=True)  6.32 us
  transfers between devices with their start and end apart: 6, of which 5 were waited for; matrix products, arithmetic and copies ran while one was open for 4% of the time, Pallas kernels for 0%

commit v1 on v0

v1 whole, which is shorter than its diff:
```python
import functools

import jax
import jax.numpy as jnp
from jax import lax
from jax.experimental import pallas as pl
from jax.experimental.pallas import tpu as pltpu
from jax.sharding import PartitionSpec as P

VMEM_BYTES = 48 * 2**20
UNROLLED = 3
FIRST_OVER = 2


def round_bound(line, owned, terms):
    most = min(terms, owned)
    for hop in range(2, line):
        most = max(min(terms, owned * hop), most + 1)
    return max(most, FIRST_OVER) + terms


def plan_kernel(line, owned, terms, rounds, lead_ref, trail_ref, table_ref, length_ref):
    count = line * owned
    shape = (line, count)
    ids = lax.broadcasted_iota(jnp.int32, shape, 1)
    place = lax.broadcasted_iota(jnp.int32, shape, 0)
    home = ids // owned
    lowest, highest = home, home
    wanted = jnp.zeros(shape, jnp.float32)
    for t in range(terms):
        a, b = lead_ref[t], trail_ref[t]
        first_home, second_home = a // owned, b // owned
        other = jnp.where(ids == a, second_home, jnp.where(ids == b, first_home, home))
        lowest = jnp.minimum(lowest, other)
        highest = jnp.maximum(highest, other)
        wanted = jnp.where((place == first_home) & (ids == b) & (home != place), 1.0, wanted)

    def pick(score):
        best = jnp.max(score, axis=1, keepdims=True)
        chosen = jnp.where((score == best) & (score > 0.0), 1.0, 0.0)
        return best, chosen, jnp.sum(chosen * (ids - count).astype(jnp.float32), axis=1, keepdims=True) + float(count)

    def anywhere(chosen):
        return jnp.max(chosen, axis=0, keepdims=True).astype(jnp.int32)

    left, right = home, home
    lane = lax.broadcasted_iota(jnp.int32, (line, 2), 1)
    length = jnp.zeros((line, 2), jnp.int32)
    for step in range(rounds):
        to_go = jnp.where((left == place) & (lowest < place), place - lowest, 0)
        best_left, moved_left, send_left = pick(jnp.where(to_go > 0, (to_go + 1) * count - ids, 0).astype(jnp.float32))
        to_go = jnp.where((right == place) & (highest > place), highest - place, 0)
        best_right, moved_right, send_right = pick(jnp.where(to_go > 0, (to_go + 1) * count - ids, 0).astype(jnp.float32))
        busy_line = jnp.max(jnp.maximum(best_left, best_right), axis=0, keepdims=True)
        if step >= FIRST_OVER:
            here = ((left <= place) & (place < home)) | ((right >= place) & (place > home))
            best_over, moved_over, send_over = pick(jnp.where(here, wanted * (count - ids).astype(jnp.float32), 0.0))
            wanted = wanted - moved_over
            busy = jnp.maximum(busy_line, jnp.max(best_over, axis=0, keepdims=True))
        else:
            send_over, busy = jnp.full((line, 1), float(count), jnp.float32), busy_line
        for i, send in enumerate((send_left, send_right, send_over)):
            table_ref[3 * step + i] = send.astype(jnp.int32)
        left = left - anywhere(moved_left)
        right = right + anywhere(moved_right)
        length = jnp.where(jnp.where(lane == 0, busy_line, busy) > 0.0, step + 1, length)
    length_ref[...] = length


def plan_rounds(leading, trailing, line, owned, rounds):
    tables, lengths = pl.pallas_call(
        functools.partial(plan_kernel, line, owned, leading.shape[0], rounds),
        out_shape=[
            jax.ShapeDtypeStruct((3 * rounds, line, 1), jnp.int32),
            jax.ShapeDtypeStruct((line, 2), jnp.int32),
        ],
        in_specs=[pl.BlockSpec(memory_space=pltpu.SMEM)] * 2,
        out_specs=[pl.BlockSpec(memory_space=pltpu.VMEM)] * 2,
        cost_estimate=pl.CostEstimate(flops=1000, bytes_accessed=1000, transcendentals=0),
    )(leading, trailing)
    return tables.reshape(rounds, 3, line), lengths[0]


def split(value):
    high = value.astype(jnp.bfloat16)
    return high, (value - high.astype(jnp.float32)).astype(jnp.bfloat16)


def dot3(left, right):
    dot = functools.partial(jnp.dot, preferred_element_type=jnp.float32)
    return dot(left[0], right[0]) + (dot(left[0], right[1]) + dot(left[1], right[0]))


def product(left, right):
    return (
        dot3(left[0], right[0]) - dot3(left[1], right[1]),
        dot3(left[0], right[1]) + dot3(left[1], right[0]),
    )


def pair(high_ref, low_ref, n):
    return [(high_ref[n, c], low_ref[n, c]) for c in range(2)]


def put(high_ref, low_ref, n, c, rows, cols, value):
    high, low = split(value)
    high_ref[n, c, rows, cols] = high
    low_ref[n, c, rows, cols] = low


def block(index, size):
    return pl.ds(pl.multiple_of(index * size, size), size)


def mix_kernel(subs, items, weight_u_ref, weight_v_ref, weight_x_ref, *refs):
    own, across = refs[0], refs[1:subs]
    arrived, over = refs[subs : subs + items], refs[subs + items : 2 * subs + items - 1]
    u_ref, v_ref, x_refs = refs[2 * subs + items - 1], refs[2 * subs + items], refs[2 * subs + items + 1 :]
    owned = own.shape[1]
    for c in range(2):
        nodes = [own[c, m] for m in range(owned)] + [a[c] for a in arrived]
        for n in range(owned):
            u_ref[n, c] = sum(weight_u_ref[n, k] * node for k, node in enumerate(nodes))
            v_ref[n, c] = sum(weight_v_ref[n, k] * node for k, node in enumerate(nodes))
        for j in range(subs - 1):
            nodes = [across[j][c, m] for m in range(owned)] + [over[j][c]]
            for n in range(owned):
                x_refs[j][n, c] = sum(weight_x_ref[n, k] * node for k, node in enumerate(nodes))


def sum_kernel(subs, reps, where_ref, *refs):
    own, beside, across = refs[0], refs[1:reps], refs[reps : reps + subs - 1]
    u, v = refs[reps + subs - 1 : reps + 2 * subs - 1], refs[reps + 2 * subs - 1 : 2 * reps + 2 * subs - 1]
    out_ref, row_high, row_low, col_high, col_low, v_high, v_low, u_high, u_low = refs[2 * reps + 2 * subs - 1 :]
    rows, cols = out_ref.shape[2:]
    every = slice(None)
    for n in range(out_ref.shape[0]):
        for c in range(2):
            for i in range(reps):
                at = block(where_ref[subs + i], cols)
                put(row_high, row_low, n, c, every, at, (own if i == 0 else beside[i - 1])[c, n])
                put(v_high, v_low, n, c, every, at, v[i][n, c])
            for i in range(subs):
                at = block(where_ref[i], rows)
                put(col_high, col_low, n, c, at, every, (own if i == 0 else across[i - 1])[c, n])
                put(u_high, u_low, n, c, at, every, u[i][n, c])
        one = product(pair(row_high, row_low, n), pair(u_high, u_low, n))
        two = product(pair(v_high, v_low, n), pair(col_high, col_low, n))
        out_ref[n, 0] = one[0] + two[0]
        out_ref[n, 1] = one[1] + two[1]


def late_kernel(subs, where_ref, weight_ref, sum_ref, row_high, row_low, *refs):
    over, out_ref = refs[: subs - 1], refs[subs - 1]
    rows = sum_ref.shape[2]
    depth = row_high.shape[3] // subs
    for n in range(sum_ref.shape[0]):
        real, imag = sum_ref[n, 0], sum_ref[n, 1]
        for j in range(subs - 1):
            at = block(where_ref[1 + j], depth)
            left = [(row_high[n, c, :, at], row_low[n, c, :, at]) for c in range(2)]
            one = product(left, [split(weight_ref[n] * over[j][c]) for c in range(2)])
            real, imag = real + one[0], imag + one[1]
        out_ref[n, 0] = real
        out_ref[n, 1] = imag


def last_kernel(reps, cells, where_ref, pick_ref, col_high, col_low, *refs):
    s, (out_ref, s_high, s_low) = refs[:reps], refs[reps:]
    cols = out_ref.shape[3]
    for n in range(out_ref.shape[1]):
        for c in range(2):
            for i in range(reps):
                put(s_high, s_low, n, c, slice(None), block(where_ref[cells + i], cols), s[i][n, c])
        real, imag = product(pair(s_high, s_low, n), pair(col_high, col_low, pick_ref[n]))
        out_ref[0, n] = real
        out_ref[1, n] = imag


def call(kernel, scalars, arrays, outs, scratch=(), flops=0):
    moved = sum(a.size * a.dtype.itemsize for a in arrays)
    return pl.pallas_call(
        kernel,
        out_shape=outs,
        in_specs=[pl.BlockSpec(memory_space=pltpu.SMEM)] * len(scalars)
        + [pl.BlockSpec(memory_space=pltpu.VMEM)] * len(arrays),
        out_specs=jax.tree.map(lambda _: pl.BlockSpec(memory_space=pltpu.VMEM), outs),
        scratch_shapes=list(scratch),
        compiler_params=pltpu.CompilerParams(vmem_limit_bytes=VMEM_BYTES),
        cost_estimate=pl.CostEstimate(flops=flops, bytes_accessed=moved, transcendentals=0),
    )(*scalars, *arrays)


def shifts(array, axis):
    size = lax.axis_size(axis)
    return [lax.ppermute(array, axis, [(i, (i + j) % size) for i in range(size)]) for j in range(1, size)]


def places(axis):
    size = lax.axis_size(axis)
    return [(lax.axis_index(axis) - j) % size for j in range(size)]


def choose(index, nodes):
    value = nodes[0][1]
    for name, array in nodes[1:]:
        value = jnp.where(index == name, array, value)
    return value


def body(meson_nodes, term_nodes, weight_codes, resident_pick):
    line = lax.axis_size("node")
    subs, reps = lax.axis_size("sub"), lax.axis_size("rep")
    _, owned, rows, cols = meson_nodes.shape
    count = owned * line
    terms = term_nodes.shape[0]
    me = lax.axis_index("node")
    base = me * owned
    leading, trailing = term_nodes[:, 0], term_nodes[:, 1]
    to_left = [(z + 1, z) for z in range(line - 1)]
    to_right = [(z, z + 1) for z in range(line - 1)]

    tables, length = plan_rounds(leading, trailing, line, owned, round_bound(line, owned, terms))
    edges = jnp.pad(tables, ((0, 0), (0, 0), (1, 1)), constant_values=count)
    mine = lax.dynamic_slice_in_dim(edges, me, 3, axis=2)

    fixed = min(line - 1, UNROLLED)
    seen = [(base + m, meson_nodes[:, m]) for m in range(owned)]
    came = []
    over, across, beside = [], None, None
    for step in range(fixed):
        sent = [choose(mine[step, i, 1], seen) for i in range(2)]
        if step >= FIRST_OVER:
            sent.append(choose(mine[step, 2, 1], came))
        sent = lax.optimization_barrier(tuple(sent))
        from_right = lax.ppermute(sent[0], "node", to_left)
        from_left = lax.ppermute(sent[1], "node", to_right)
        if step >= FIRST_OVER:
            over.append(shifts(sent[2], "sub"))
        if step == 0:
            across, beside = shifts(meson_nodes, "sub"), shifts(meson_nodes, "rep")
            for other in shifts(length, "grp"):
                length = jnp.maximum(length, other)
        new = [(mine[step, 0, 2], from_right), (mine[step, 1, 0], from_left)]
        came = came + new
        seen = seen + new

    factors = (weight_codes.astype(jnp.float32) - 3.5) * 0.5
    mine_ids = base + jnp.arange(owned, dtype=jnp.int32)
    first_mine = factors[:, None] * (leading[:, None] == mine_ids)
    second_mine = factors[:, None] * (trailing[:, None] == mine_ids)

    def weights(mine_terms, others, names):
        return jnp.sum(mine_terms[:, :, None] * (others[:, None] == names)[:, None, :], axis=0)

    own_names = [base + m for m in range(owned)]
    names = jnp.stack(own_names + [name for name, _ in came])
    weight_u = weights(first_mine, trailing, names)
    weight_v = weights(second_mine, leading, names)
    weight_x = weights(first_mine, trailing, jnp.stack(own_names + [mine[step, 2, 1] for step in range(FIRST_OVER, fixed)]))
    where = jnp.stack([*places("sub"), *places("rep")]).astype(jnp.int32)
    picks = lax.dynamic_slice_in_dim(resident_pick, base, owned)
    nodes_shape = (owned, 2, rows, cols)
    depth = rows * subs
    flops = 3 * 8 * owned * rows * depth * cols

    def out(shape, dtype=jnp.float32):
        return jax.ShapeDtypeStruct(shape, dtype)

    def mixed():
        return call(
            functools.partial(mix_kernel, subs, len(came)),
            [weight_u, weight_v, weight_x],
            [meson_nodes, *across, *[array for _, array in came], *over[0]],
            [out(nodes_shape)] * (subs + 1),
        )

    def sums(u, v):
        row_part, col_part = (owned, 2, rows, depth), (owned, 2, depth, cols)
        scratch = [pltpu.VMEM(row_part, jnp.bfloat16)] * 2 + [pltpu.VMEM(col_part, jnp.bfloat16)] * 2
        return call(
            functools.partial(sum_kernel, subs, reps),
            [where],
            [meson_nodes, *beside, *across, *u, v, *shifts(v, "rep")],
            [out(nodes_shape)] + [out(row_part, jnp.bfloat16)] * 2 + [out(col_part, jnp.bfloat16)] * 2,
            scratch,
            2 * flops,
        )

    def finish(summed, col_high, col_low):
        scratch = [pltpu.VMEM((owned, 2, rows, depth), jnp.bfloat16)] * 2
        return call(
            functools.partial(last_kernel, reps, subs),
            [where, picks],
            [col_high, col_low, summed, *shifts(summed, "rep")],
            out(meson_nodes.shape),
            scratch,
            flops,
        )

    def short(_):
        index = mine[fixed, 2, 1]
        late = shifts(choose(index, came), "sub")
        u, v, *ux = mixed()
        summed, row_high, row_low, col_high, col_low = sums([u, *ux], v)
        weight_late = weights(first_mine, trailing, index[None])[:, 0]
        summed = call(
            functools.partial(late_kernel, subs),
            [where, weight_late],
            [summed, row_high, row_low, *late],
            out(nodes_shape),
            flops=flops // subs,
        )
        return finish(summed, col_high, col_low)

    def long(_):
        u, v, *ux = mixed()
        held = jnp.zeros((count + 1, 2, rows, cols), jnp.float32)
        for name, array in seen:
            held = lax.dynamic_update_slice_in_dim(held, array[None], name, 0)

        def add(total, mine_terms, others, name, item):
            return total + weights(mine_terms, others, name[None])[:, :, None, None] * item[None]

        def more(state):
            return state[0] < length[1]

        def again(state):
            step, held, u, v = state
            ids = lax.dynamic_index_in_dim(mine, step, 0, keepdims=False)
            left, right, item = lax.optimization_barrier(
                tuple(lax.dynamic_index_in_dim(held, ids[i, 1], 0, keepdims=False) for i in range(3))
            )
            from_right = lax.ppermute(left, "node", to_left)
            from_left = lax.ppermute(right, "node", to_right)
            items = [item, *shifts(item, "sub")]
            from_right, from_left = lax.optimization_barrier((from_right, from_left))
            u = [add(total, first_mine, trailing, ids[2, 1], x) for total, x in zip(u, items)]
            v = add(v, second_mine, leading, ids[0, 2], from_right)
            v = add(v, second_mine, leading, ids[1, 0], from_left)
            held = lax.dynamic_update_slice_in_dim(held, from_right[None], ids[0, 2], 0)
            held = lax.dynamic_update_slice_in_dim(held, from_left[None], ids[1, 0], 0)
            return step + 1, held, u, v

        gone = weights(first_mine, trailing, jnp.stack([mine[step, 2, 1] for step in range(FIRST_OVER, fixed)]))
        start = [
            sum(
                weight[:, k, None, None, None] * node[None]
                for weight, nodes in ((weight_u, [meson_nodes[:, m] for m in range(owned)]), (gone, [choose(mine[FIRST_OVER, 2, 1], came)]))
                for k, node in enumerate(nodes)
            ),
            *ux,
        ]
        _, _, u, v = lax.while_loop(more, again, (jnp.int32(fixed), held, start, v))
        summed, _, _, col_high, col_low = sums(u, v)
        return finish(summed, col_high, col_low)

    is_short = (length[0] <= fixed) & (length[1] <= fixed + 1)
    return lax.cond(is_short, short, long, None)


def solution(mesh):
    in_specs = (P(None, ("grp", "node"), "sub", "rep"), P("grp", None), P("grp"), P("grp"))
    out_specs = P(None, ("grp", "node"), "sub", "rep")
    return jax.shard_map(body, mesh=mesh, in_specs=in_specs, out_specs=out_specs, check_vma=False)
```

time: 192 us -> 118 us (0.61)
  waiting for transfers between devices: 77.2 us -> 19.8 us
  blocking collectives: 55.5 us -> 0 us
  Pallas kernels: 0 us -> 17.2 us
  matrix products: 14.4 us -> 0 us
  starting transfers between devices: 11.4 us -> 23.8 us
  between operations: 13.4 us -> 24.3 us
  loops' own time: 0 us -> 6.06 us
  other arithmetic: 4.75 us -> 9.05 us
  local copies, waits for them, and re-layouts: 15.1 us -> 17.1 us
    all_to_all x2 -> x0, blocking collectives: 55.5 us -> none  [the longest x1 27.8 us: body(): lax.all_to_all(summed.reshape(2, total_nodes, 1, band * col_count), 'node...]
    all_gather x4 -> x0, waiting for transfers between devices: 40.1 us -> none  [the longest x1 19.8 us: body(): lax.all_gather(right_band, 'sub', axis=2, tiled=True)]
    all_to_all x2 -> x0, waiting for transfers between devices: 36.3 us -> none  [the longest x1 24.2 us: body(): lax.all_to_all(banded, 'node', split_axis=2, concat_axis=1, tiled=True)]
    ppermute x0 -> x13, starting transfers between devices: none -> 23.8 us  [the longest x3 14.2 us: body(): from_left = lax.ppermute(sent[1], 'node', to_right)]
    ppermute x0 -> x13, waiting for transfers between devices: none -> 19.8 us  [the longest x7 10.5 us: shifts(): lax.ppermute(array, axis, [(i, (i + j) % size) for i in range(size)])]
    pallas_call x0 -> x5, Pallas kernels: none -> 17.2 us  [the longest x4 14.9 us: call(): pl.pallas_call(kernel, out_shape=outs, in_specs=[pl.BlockSpec(memory_spac...]
    dot_general x9 -> x0, matrix products: 14.4 us -> none  [the longest x2 4.7 us: complex_step(): jnp.einsum('kij,kjl->kil', full_left[0], segment[1], precision=highest, p...]
    all_to_all x2 -> x0, starting transfers between devices: 11.2 us -> none  [the longest x1 6.32 us: body(): lax.all_to_all(banded, 'node', split_axis=2, concat_axis=1, tiled=True)]
  transfers between devices with their start and end apart: 6 -> 13, of which waited for: 5 -> 7; matrix products, arithmetic and copies ran while one was open for 4% -> 16% of each run, Pallas kernels for 0% -> 8%
where the time goes in v1:
time: 118 us; the launch traced here: 117 us
  between operations  24.3 us (21%)
  starting transfers between devices  23.8 us (20%)
  waiting for transfers between devices  19.8 us (17%)
  Pallas kernels  17.2 us (15%)
  local copies, waits for them, and re-layouts  17.1 us (14%)
  other arithmetic  9.05 us (8%)
  loops' own time  6.06 us (5%)
    pallas_call x4, Pallas kernels, call(): pl.pallas_call(kernel, out_shape=outs, in_specs=[pl.BlockSpec(memory_spac...  14.9 us
    ppermute x3, starting transfers between devices, body(): from_left = lax.ppermute(sent[1], 'node', to_right)  14.2 us
    ppermute x7, waiting for transfers between devices, shifts(): lax.ppermute(array, axis, [(i, (i + j) % size) for i in range(size)])  10.5 us
    ppermute x3, waiting for transfers between devices, body(): from_right = lax.ppermute(sent[0], 'node', to_left)  6.96 us
    another operation x1, loops' own time, body(): return lax.cond(is_short, short, long, None)  6.06 us
    cond x16, local copies, waits for them, and re-layouts  5.83 us
    ppermute x7, starting transfers between devices, shifts(): lax.ppermute(array, axis, [(i, (i + j) % size) for i in range(size)])  5.75 us
    select_n x5, other arithmetic, choose(): value = jnp.where(index == name, array, value)  5.25 us
  transfers between devices with their start and end apart: 13, of which 7 were waited for; matrix products, arithmetic and copies ran while one was open for 16% of the time, Pallas kernels for 8%

profile of v1, /device:TPU:0, one launch (start us, length us, event | category | flops | bytes accessed | tf_op | source)
XLA Modules:
  0.0 117.3 jit_solution(12255665808956725004)
XLA Ops:
  0.0 2.9 %collective-permute-start.15 = (f32[2,2,256,256]{3,2,1,0:T(8,128)}, f32[2,2,256,256]{3,2,1,0:T(8,128)}, u32[]{:S(2)}, u32[]{:S(2)}) collective-permute-start(f32[2,2,256,256]{3,2,1,0:T(8,128)} %param.8), channel_id=1, source_target_pairs={{0,2},{2,0},{1,3},{3,1},{4,6},{6,4},{5,7},{7,5},{8,10},{10,8},{9,1... | collective-permute-start | bytes 3145736 | tf_op jit(solution)/shard_map/ppermute | solution.py:196
  2.9 1.3 %fusion.15 = (s32[4,1]{0,1:T(1,128)S(1)}, s32[4]{0:T(128)}, s32[4]{0:T(128)S(1)}, s32[4,1]{0,1:T(1,128)S(1)}) fusion(s32[4,2]{0,1:T(2,128)} %param.9), kind=kLoop, calls=%fused_computation.88 | loop fusion | bytes 96 | tf_op jit(solution)/shard_map/slice | solution.py:219
  4.3 2.3 %shard_map.48 = (s32[27,4,1]{2,1,0:T(4,128)}, s32[4,2]{1,0:T(4,128)}) custom-call(s32[4]{0:T(128)} %get-tuple-element.514.lead_ref, s32[4]{0:T(128)S(1)} %get-tuple-element.515.trail_ref), custom_call_target="tpu_custom_call" | custom-call | flops 1000 | bytes 1000 | tf_op jit(solution)/shard_map/pallas_call | solution.py:71
  7.3 1.5 %collective-permute-start.8 = (s32[2]{0:T(128)S(1)}, s32[2]{0:T(128)S(1)}, u32[]{:S(2)}, u32[]{:S(2)}) collective-permute-start(s32[2]{0:T(128)S(1)} %slice_bitcast_fusion.4), channel_id=1, source_target_pairs={{0,16},{16,0},{1,17},{17,1},{2,18},{18,2},{3,19},{19,3},{4,20},{20... | collective-permute-start | bytes 32 | tf_op jit(solution)/shard_map/ppermute | solution.py:196
  11.9 1.3 %select_bitcast_fusion = (f32[2,256,256]{2,1,0:T(8,128)S(1)}, f32[2,256,256]{2,1,0:T(8,128)S(1)}) fusion(pred[]{:T(512)S(6)} %eq.258, f32[2,2,256,256]{3,2,1,0:T(8,128)} %param.8, pred[]{:T(512)S(6)} %eq.257), kind=kLoop, calls=%fused_computation.53 | loop fusion | flops 262144 | bytes 2097154 | tf_op jit(solution)/shard_map/jit(_where)/select_n | solution.py:207
  13.2 1.3 %collective-permute-start.9 = (f32[2,256,256]{2,1,0:T(8,128)S(1)}, f32[2,256,256]{2,1,0:T(8,128)S(1)}, u32[]{:S(2)}, u32[]{:S(2)}) collective-permute-start(f32[2,256,256]{2,1,0:T(8,128)S(1)} %get-tuple-element.271), channel_id=1, source_target_pairs={{4,0},{8,4},{12,8},{5,1},{9,5},{13,9},{6,2},{10,6},{14,10},{7,3},{... | collective-permute-start | bytes 1572872 | tf_op jit(solution)/shard_map/ppermute | solution.py:236
  14.5 4.6 %collective-permute-start.10 = (f32[2,256,256]{2,1,0:T(8,128)S(1)}, f32[2,256,256]{2,1,0:T(8,128)S(1)}, u32[]{:S(2)}, u32[]{:S(2)}) collective-permute-start(f32[2,256,256]{2,1,0:T(8,128)S(1)} %get-tuple-element.272), channel_id=1, source_target_pairs={{0,4},{4,8},{8,12},{1,5},{5,9},{9,13},{2,6},{6,10},{10,14},{3,7},{... | collective-permute-start | bytes 1572872 | tf_op jit(solution)/shard_map/ppermute | solution.py:237
  27.6 1.6 %collective-permute-done.9 = f32[2,256,256]{2,1,0:T(8,128)S(1)} collective-permute-done((f32[2,256,256]{2,1,0:T(8,128)S(1)}, f32[2,256,256]{2,1,0:T(8,128)S(1)}, u32[]{:S(2)}, u32[]{:S(2)}) %collective-permute-start.9) | collective-permute-done | bytes 524320 | tf_op jit(solution)/shard_map/ppermute | solution.py:236
  30.3 2.3 %fusion.11 = (f32[2,256,256]{2,1,0:T(8,128)}, f32[2,256,256]{2,1,0:T(8,128)}) fusion(f32[2,256,256]{2,1,0:T(8,128)S(1)} %collective-permute-done.10, f32[2,256,256]{2,1,0:T(8,128)S(1)} %collective-permute-done.9, pred[]{:T(512)S(6)} %eq.264, pred[]{:T(512)S(6)} %eq.263, pred[]{:T(512)S(6)} %eq.262, f32[2,2,256,256]{3,2,1,0:T(8,128)} %param.8, pred[]{:T(512)S(6)} %eq.261, ...), kind=kLoop, calls=%fused_computation.49 | loop fusion | flops 786432 | bytes 3145734 | tf_op jit(solution)/shard_map/jit(_where)/select_n | solution.py:207
  32.6 1.3 %collective-permute-start.11 = (f32[2,256,256]{2,1,0:T(8,128)}, f32[2,256,256]{2,1,0:T(8,128)S(1)}, u32[]{:S(2)}, u32[]{:S(2)}) collective-permute-start(f32[2,256,256]{2,1,0:T(8,128)} %get-tuple-element.273), channel_id=1, source_target_pairs={{4,0},{8,4},{12,8},{5,1},{9,5},{13,9},{6,2},{10,6},{14,10},{7,3},{... | collective-permute-start | bytes 1572872 | tf_op jit(solution)/shard_map/ppermute | solution.py:236
  33.9 5.0 %collective-permute-start.12 = (f32[2,256,256]{2,1,0:T(8,128)}, f32[2,256,256]{2,1,0:T(8,128)S(1)}, u32[]{:S(2)}, u32[]{:S(2)}) collective-permute-start(f32[2,256,256]{2,1,0:T(8,128)} %get-tuple-element.274), channel_id=1, source_target_pairs={{0,4},{4,8},{8,12},{1,5},{5,9},{9,13},{2,6},{6,10},{10,14},{3,7},{... | collective-permute-start | bytes 1572872 | tf_op jit(solution)/shard_map/ppermute | solution.py:237
  54.5 3.9 %stack.31 = s32[8]{0:T(128)S(1)} concatenate(s32[1]{0:T(128)} %bitcast.52, s32[1]{0:T(128)} %bitcast.53, s32[1]{0:T(128)} %bitcast.54, s32[1]{0:T(128)} %bitcast.55, s32[1]{0:T(128)} %bitcast.56, s32[1]{0:T(128)} %bitcast.57, s32[1]{0:T(128)} %bitcast.58, s32[1]{0:T(128)} %bitcast.59), dimensions={0} | concatenate | bytes 64 | tf_op jit(solution)/shard_map/stack | solution.py:257
  59.8 1.3 %collective-permute-start.13 = (f32[2,256,256]{2,1,0:T(8,128)S(1)}, f32[2,256,256]{2,1,0:T(8,128)S(1)}, u32[]{:S(2)}, u32[]{:S(2)}) collective-permute-start(f32[2,256,256]{2,1,0:T(8,128)S(1)} %get-tuple-element.275), channel_id=1, source_target_pairs={{4,0},{8,4},{12,8},{5,1},{9,5},{13,9},{6,2},{10,6},{14,10},{7,3},{... | collective-permute-start | bytes 1572872 | tf_op jit(solution)/shard_map/ppermute | solution.py:236
  61.1 4.6 %collective-permute-start.14 = (f32[2,256,256]{2,1,0:T(8,128)S(1)}, f32[2,256,256]{2,1,0:T(8,128)S(1)}, u32[]{:S(2)}, u32[]{:S(2)}) collective-permute-start(f32[2,256,256]{2,1,0:T(8,128)S(1)} %get-tuple-element.276), channel_id=1, source_target_pairs={{0,4},{4,8},{8,12},{1,5},{5,9},{9,13},{2,6},{6,10},{10,14},{3,7},{... | collective-permute-start | bytes 1572872 | tf_op jit(solution)/shard_map/ppermute | solution.py:237
  69.0 5.4 %collective-permute-done.13 = f32[2,256,256]{2,1,0:T(8,128)S(1)} collective-permute-done((f32[2,256,256]{2,1,0:T(8,128)S(1)}, f32[2,256,256]{2,1,0:T(8,128)S(1)}, u32[]{:S(2)}, u32[]{:S(2)}) %collective-permute-start.13) | collective-permute-done | bytes 524320 | tf_op jit(solution)/shard_map/ppermute | solution.py:236
  75.5 2.3 %collective-permute-done.16 = f32[2,256,256]{2,1,0:T(8,128)S(1)} collective-permute-done((f32[2,256,256]{2,1,0:T(8,128)S(1)}, f32[2,256,256]{2,1,0:T(8,128)S(1)}, u32[]{:S(2)}, u32[]{:S(2)}) %collective-permute-start.16) | collective-permute-done | bytes 524320 | tf_op jit(solution)/shard_map/ppermute | solution.py:196
  77.9 38.4 %conditional.1 = (f32[2,2,256,256]{3,2,1,0:T(8,128)S(1)}) conditional(s32[]{:T(128)} %bitcast.32, (f32[2,1,256,256]{3,2,0,1:T(8,128)}, s32[]{:T(128)}, f32[2,1,256,256]{3,2,0,1:T(8,128)}, s32[]{:T(128)}, f32[2,256,256]{2,1,0:T(8,128)S(1)}, /*index=5*/s32[]{:T(128)}, f32[2,256,256]{2,1,0:T(8,128)S(1)}, s32[]{:T(128)}, f32[2,256,256]{2,1,0:T(8,128)S(1)}, ...), branch_computations={%region_3.10_spmd, %region_10.12_spmd} | conditional | flops 5637799936 | bytes 109054792 | solution.py:359
  82.1 3.2 %branch_1_fun.4 = (f32[2,2,256,256]{3,2,1,0:T(8,128)S(1)}, f32[2,2,256,256]{3,2,1,0:T(8,128)S(1)}, f32[2,2,256,256]{3,2,1,0:T(8,128)S(1)}) custom-call(f32[2,8]{1,0:T(2,128)S(1)} %get-tuple-element.234.weight_u_ref, f32[2,8]{1,0:T(2,128)S(1)} %get-tuple-element.235.weight_v_ref, f32[2,3]{1,0:T(2,128)S(1)} %copy.28.weight_x_ref, ...), custom_call_target="tpu_custom_call" | custom-call | bytes 5767168 | tf_op jit(solution)/shard_map/cond/branch_1_fun/pallas_call | solution.py:182
  93.9 1.3 %select_select_fusion = f32[2,256,256]{2,1,0:T(8,128)S(1)} fusion(f32[2,256,256]{2,1,0:T(8,128)} %copy-done.15, f32[2,256,256]{2,1,0:T(8,128)} %copy-done.12, f32[2,256,256]{2,1,0:T(8,128)} %copy-done.9, f32[2,256,256]{2,1,0:T(8,128)} %copy-done.8, f32[2,256,256]{2,1,0:T(8,128)S(1)} %get-tuple-element.238.refs_3_, ...), kind=kLoop, calls=%fused_computation.18 | loop fusion | flops 655360 | bytes 3670021 | tf_op jit(solution)/shard_map/cond/branch_1_fun/jit(_where)/select_n | solution.py:207
  96.4 7.4 %branch_1_fun.5 = (f32[2,2,256,256]{3,2,1,0:T(8,128)S(1)}, bf16[2,2,256,512]{3,2,1,0:T(8,128)(2,1)S(1)}, bf16[2,2,256,512]{3,2,1,0:T(8,128)(2,1)S(1)}, bf16[2,2,...) custom-call(s32[4]{0:T(128)S(1)} %get-tuple-element.229.where_ref, ...), custom_call_target="tpu_custom_call" | custom-call | flops 3221225472 | bytes 7340032 | tf_op jit(solution)/shard_map/cond/branch_1_fun/pallas_call | solution.py:182
  103.9 5.5 %collective-permute-done.1.refs_0_ = f32[2,256,256]{2,1,0:T(8,128)S(1)} collective-permute-done((f32[2,256,256]{2,1,0:T(8,128)S(1)}, f32[2,256,256]{2,1,0:T(8,128)S(1)}, u32[]{:S(2)}, u32[]{:S(2)}) %collective-permute-start.1) | collective-permute-done | bytes 524320 | tf_op jit(solution)/shard_map/cond/branch_1_fun/ppermute | solution.py:196
  109.4 1.6 %branch_1_fun.6.refs_0_ = f32[2,2,256,256]{3,2,1,0:T(8,128)S(1)} custom-call(s32[4]{0:T(128)S(1)} %get-tuple-element.229.where_ref, f32[2]{0:T(128)S(1)} %multiply_reduce_fusion.3.weight_ref, f32[2,2,256,256]{3,2,1,0:T(8,128)S(1)} %get-tuple-element.252.sum_ref, bf16[2,2,256,512]{3,2,1,0:T(8,128)(2,1)S(1)} %get-tuple-element.253.row_high, ...), custom_call_target="tpu_custom_call" | custom-call | flops 805306368 | bytes 3670016 | tf_op jit(solution)/shard_map/cond/branch_1_fun/pallas_call | solution.py:182
  111.1 2.6 %collective-permute-done.2.refs_1_ = f32[2,2,256,256]{3,2,1,0:T(8,128)S(1)} collective-permute-done((f32[2,2,256,256]{3,2,1,0:T(8,128)S(1)}, f32[2,2,256,256]{3,2,1,0:T(8,128)S(1)}, u32[]{:S(2)}, u32[]{:S(2)}) %collective-permute-start.2) | collective-permute-done | bytes 1048608 | tf_op jit(solution)/shard_map/cond/branch_1_fun/ppermute | solution.py:196
  113.7 2.7 %branch_1_fun.7 = f32[2,2,256,256]{3,2,1,0:T(8,128)S(1)} custom-call(s32[4]{0:T(128)S(1)} %get-tuple-element.229.where_ref, s32[2]{0:T(128)S(1)} %get-tuple-element.230.pick_ref, bf16[2,2,512,256]{3,2,1,0:T(8,128)(2,1)S(1)} %get-tuple-element.247.col_high, bf16[2,2,512,256]{3,2,1,0:T(8,128)(2,1)S(1)} %get-tuple-element.248.col_low, ...), custom_call_target="tpu_custom_call" | custom-call | flops 1610612736 | bytes 4194304 | tf_op jit(solution)/shard_map/cond/branch_1_fun/pallas_call | solution.py:182
  (65 shorter events, 19.7 us)
Async XLA Ops:
  0.0 58.4 %copy-start.3 = (f32[2,2,256,256]{3,2,1,0:T(8,128)S(1)}, f32[2,2,256,256]{3,2,1,0:T(8,128)}, u32[]{:S(2)}) copy-start(f32[2,2,256,256]{3,2,1,0:T(8,128)} %param.8) | copy-start | bytes 3145732
  0.0 54.4 %copy-start.26 = (s32[8]{0:T(128)S(1)}, s32[8]{0:T(128)}, u32[]{:S(2)}) copy-start(s32[8]{0:T(128)} %param.11) | copy-start | bytes 100
  0.0 68.9 %collective-permute-start.15 = (f32[2,2,256,256]{3,2,1,0:T(8,128)}, f32[2,2,256,256]{3,2,1,0:T(8,128)}, u32[]{:S(2)}, u32[]{:S(2)}) collective-permute-start(f32[2,2,256,256]{3,2,1,0:T(8,128)} %param.8), channel_id=1, source_target_pairs={{0,2},{2,0},{1,3},{3,1},{4,6},{6,4},{5,7},{7,5},{8,10},{10,8},{9,1... | collective-permute-start | bytes 3145736 | tf_op jit(solution)/shard_map/ppermute | solution.py:196
  2.9 66.0 %collective-permute-start.17 = (f32[2,2,256,256]{3,2,1,0:T(8,128)}, f32[2,2,256,256]{3,2,1,0:T(8,128)}, u32[]{:S(2)}, u32[]{:S(2)}) collective-permute-start(f32[2,2,256,256]{3,2,1,0:T(8,128)} %param.8), channel_id=1, source_target_pairs={{0,1},{1,0},{2,3},{3,2},{4,5},{5,4},{6,7},{7,6},{8,9},{9,8},{10,11... | collective-permute-start | bytes 3145736 | tf_op jit(solution)/shard_map/ppermute | solution.py:196
  4.3 54.0 %copy-start.23 = (s32[4]{0:T(128)S(1)}, s32[4]{0:T(128)}, u32[]{:S(2)}) copy-start(s32[4]{0:T(128)} %get-tuple-element.514.lead_ref) | copy-start | bytes 52
  7.3 58.4 %collective-permute-start.8 = (s32[2]{0:T(128)S(1)}, s32[2]{0:T(128)S(1)}, u32[]{:S(2)}, u32[]{:S(2)}) collective-permute-start(s32[2]{0:T(128)S(1)} %slice_bitcast_fusion.4), channel_id=1, source_target_pairs={{0,16},{16,0},{1,17},{17,1},{2,18},{18,2},{3,19},{19,3},{4,20},{20... | collective-permute-start | bytes 32 | tf_op jit(solution)/shard_map/ppermute | solution.py:196
  13.2 15.9 %collective-permute-start.9 = (f32[2,256,256]{2,1,0:T(8,128)S(1)}, f32[2,256,256]{2,1,0:T(8,128)S(1)}, u32[]{:S(2)}, u32[]{:S(2)}) collective-permute-start(f32[2,256,256]{2,1,0:T(8,128)S(1)} %get-tuple-element.271), channel_id=1, source_target_pairs={{4,0},{8,4},{12,8},{5,1},{9,5},{13,9},{6,2},{10,6},{14,10},{7,3},{... | collective-permute-start | bytes 1572872 | tf_op jit(solution)/shard_map/ppermute | solution.py:236
  14.5 15.8 %collective-permute-start.10 = (f32[2,256,256]{2,1,0:T(8,128)S(1)}, f32[2,256,256]{2,1,0:T(8,128)S(1)}, u32[]{:S(2)}, u32[]{:S(2)}) collective-permute-start(f32[2,256,256]{2,1,0:T(8,128)S(1)} %get-tuple-element.272), channel_id=1, source_target_pairs={{0,4},{4,8},{8,12},{1,5},{5,9},{9,13},{2,6},{6,10},{10,14},{3,7},{... | collective-permute-start | bytes 1572872 | tf_op jit(solution)/shard_map/ppermute | solution.py:237
  32.6 26.8 %collective-permute-start.11 = (f32[2,256,256]{2,1,0:T(8,128)}, f32[2,256,256]{2,1,0:T(8,128)S(1)}, u32[]{:S(2)}, u32[]{:S(2)}) collective-permute-start(f32[2,256,256]{2,1,0:T(8,128)} %get-tuple-element.273), channel_id=1, source_target_pairs={{4,0},{8,4},{12,8},{5,1},{9,5},{13,9},{6,2},{10,6},{14,10},{7,3},{... | collective-permute-start | bytes 1572872 | tf_op jit(solution)/shard_map/ppermute | solution.py:236
  33.9 25.5 %collective-permute-start.12 = (f32[2,256,256]{2,1,0:T(8,128)}, f32[2,256,256]{2,1,0:T(8,128)S(1)}, u32[]{:S(2)}, u32[]{:S(2)}) collective-permute-start(f32[2,256,256]{2,1,0:T(8,128)} %get-tuple-element.274), channel_id=1, source_target_pairs={{0,4},{4,8},{8,12},{1,5},{5,9},{9,13},{2,6},{6,10},{10,14},{3,7},{... | collective-permute-start | bytes 1572872 | tf_op jit(solution)/shard_map/ppermute | solution.py:237
  59.8 14.5 %collective-permute-start.13 = (f32[2,256,256]{2,1,0:T(8,128)S(1)}, f32[2,256,256]{2,1,0:T(8,128)S(1)}, u32[]{:S(2)}, u32[]{:S(2)}) collective-permute-start(f32[2,256,256]{2,1,0:T(8,128)S(1)} %get-tuple-element.275), channel_id=1, source_target_pairs={{4,0},{8,4},{12,8},{5,1},{9,5},{13,9},{6,2},{10,6},{14,10},{7,3},{... | collective-permute-start | bytes 1572872 | tf_op jit(solution)/shard_map/ppermute | solution.py:236
  61.1 14.4 %collective-permute-start.14 = (f32[2,256,256]{2,1,0:T(8,128)S(1)}, f32[2,256,256]{2,1,0:T(8,128)S(1)}, u32[]{:S(2)}, u32[]{:S(2)}) collective-permute-start(f32[2,256,256]{2,1,0:T(8,128)S(1)} %get-tuple-element.276), channel_id=1, source_target_pairs={{0,4},{4,8},{8,12},{1,5},{5,9},{9,13},{2,6},{6,10},{10,14},{3,7},{... | collective-permute-start | bytes 1572872 | tf_op jit(solution)/shard_map/ppermute | solution.py:237
  65.7 12.1 %collective-permute-start.16 = (f32[2,256,256]{2,1,0:T(8,128)S(1)}, f32[2,256,256]{2,1,0:T(8,128)S(1)}, u32[]{:S(2)}, u32[]{:S(2)}) collective-permute-start(f32[2,256,256]{2,1,0:T(8,128)S(1)} %select_select_fusion.2), channel_id=1, source_target_pairs={{0,2},{2,0},{1,3},{3,1},{4,6},{6,4},{5,7},{7,5},{8,10},{10,8},{9,1... | collective-permute-start | bytes 1572872 | tf_op jit(solution)/shard_map/ppermute | solution.py:196
  78.1 0.8 copy-start.9
  78.9 0.8 copy-start.12
  79.7 0.8 copy-start.15
  81.3 0.8 copy-start.8
  85.3 1.0 copy-start
  86.3 1.0 copy-start.2
  87.2 9.2 %copy-start.1 = (f32[2,2,256,256]{3,2,1,0:T(8,128)}, f32[2,2,256,256]{3,2,1,0:T(8,128)S(1)}, u32[]{:S(2)}) copy-start(f32[2,2,256,256]{3,2,1,0:T(8,128)S(1)} %get-tuple-element.246.refs_5_) | copy-start | bytes 3145732 | tf_op jit(solution)/shard_map/cond
  87.3 9.2 %collective-permute-start = (f32[2,2,256,256]{3,2,1,0:T(8,128)S(1)}, f32[2,2,256,256]{3,2,1,0:T(8,128)}, u32[]{:S(2)}, u32[]{:S(2)}) collective-permute-start(f32[2,2,256,256]{3,2,1,0:T(8,128)S(1)} %get-tuple-element.246.refs_5_), channel_id=1, source_target_pairs={{0,1},{1,0},{2,3},{3,2},{4,5},{5,4},{6,7},{7,6},{8,9},{9,8},{10,11... | collective-permute-start | bytes 3145736 | tf_op jit(solution)/shard_map/cond/branch_1_fun/ppermute | solution.py:196
  95.1 14.3 %collective-permute-start.1 = (f32[2,256,256]{2,1,0:T(8,128)S(1)}, f32[2,256,256]{2,1,0:T(8,128)S(1)}, u32[]{:S(2)}, u32[]{:S(2)}) collective-permute-start(f32[2,256,256]{2,1,0:T(8,128)S(1)} %select_select_fusion), channel_id=1, source_target_pairs={{0,2},{2,0},{1,3},{3,1},{4,6},{6,4},{5,7},{7,5},{8,10},{10,8},{9,1... | collective-permute-start | bytes 1572872 | tf_op jit(solution)/shard_map/cond/branch_1_fun/ppermute | solution.py:196
  111.0 2.7 %collective-permute-start.2 = (f32[2,2,256,256]{3,2,1,0:T(8,128)S(1)}, f32[2,2,256,256]{3,2,1,0:T(8,128)S(1)}, u32[]{:S(2)}, u32[]{:S(2)}) collective-permute-start(f32[2,2,256,256]{3,2,1,0:T(8,128)S(1)} %branch_1_fun.6.refs_0_), channel_id=1, source_target_pairs={{0,1},{1,0},{2,3},{3,2},{4,5},{5,4},{6,7},{7,6},{8,9},{9,8},{10,11... | collective-permute-start | bytes 3145736 | tf_op jit(solution)/shard_map/cond/branch_1_fun/ppermute | solution.py:196
  116.4 1.0 copy-start.27
  (1 other events, 0.8 us)

commit v2 on v1

v2 whole, which is shorter than its diff:
```python
import functools

import jax
import jax.numpy as jnp
from jax import lax
from jax.experimental import pallas as pl
from jax.experimental.pallas import tpu as pltpu
from jax.sharding import PartitionSpec as P

VMEM_BYTES = 24 * 2**20
UNROLLED = 3
FIRST_OVER = 2


def round_bound(line, owned, terms):
    most = min(terms, owned)
    for hop in range(2, line):
        most = max(min(terms, owned * hop), most + 1)
    return max(most, FIRST_OVER) + terms


def plan_kernel(line, owned, terms, rounds, opened, me_ref, terms_ref, codes_ref, slot_ref, weight_ref, table_ref, length_ref):
    count = line * owned
    shape = (line, count)
    ids = lax.broadcasted_iota(jnp.int32, shape, 1)
    place = lax.broadcasted_iota(jnp.int32, shape, 0)
    home = ids // owned
    lowest, highest = home, home
    wanted = jnp.zeros(shape, jnp.float32)
    me = me_ref[0]
    even = lax.rem(me, 2) == 0
    pairs = [(terms_ref[t, 0], terms_ref[t, 1]) for t in range(terms)]
    for a, b in pairs:
        first_home, second_home = a // owned, b // owned
        other = jnp.where(ids == a, second_home, jnp.where(ids == b, first_home, home))
        lowest = jnp.minimum(lowest, other)
        highest = jnp.maximum(highest, other)
        wanted = jnp.where((place == first_home) & (ids == b) & (home != place), 1.0, wanted)

    def pick(score):
        best = jnp.max(score, axis=1, keepdims=True)
        chosen = jnp.where((score == best) & (score > 0.0), 1.0, 0.0)
        return best, chosen, jnp.sum(chosen * (ids - count).astype(jnp.float32), axis=1, keepdims=True) + float(count)

    def anywhere(chosen):
        return jnp.max(chosen, axis=0, keepdims=True).astype(jnp.int32)

    rank = lax.broadcasted_iota(jnp.int32, (line, 1), 0)

    def of(send, who):
        return jnp.sum(jnp.where(rank == who, send - float(count), 0.0), axis=0, keepdims=True).astype(jnp.int32) + count

    names = [jnp.full((1, 1), me * owned + m, jnp.int32) for m in range(owned)]

    def write(row, send):
        wanted_name = of(send, me)
        slot = jnp.zeros((1, 1), jnp.int32)
        for k, name in enumerate(names):
            slot = jnp.where(wanted_name == name, k, slot)
        slot_ref[row] = jnp.broadcast_to(slot, slot_ref.shape[1:])
        return wanted_name

    left, right = home, home
    lane = lax.broadcasted_iota(jnp.int32, (line, 2), 1)
    length = jnp.zeros((line, 2), jnp.int32)
    gone = []
    for step in range(rounds):
        to_go = jnp.where((left == place) & (lowest < place), place - lowest, 0)
        best_left, moved_left, send_left = pick(jnp.where(to_go > 0, (to_go + 1) * count - ids, 0).astype(jnp.float32))
        to_go = jnp.where((right == place) & (highest > place), highest - place, 0)
        best_right, moved_right, send_right = pick(jnp.where(to_go > 0, (to_go + 1) * count - ids, 0).astype(jnp.float32))
        busy_line = jnp.max(jnp.maximum(best_left, best_right), axis=0, keepdims=True)
        if step >= FIRST_OVER:
            here = ((left <= place) & (place < home)) | ((right >= place) & (place > home))
            best_over, moved_over, send_over = pick(jnp.where(here, wanted * (count - ids).astype(jnp.float32), 0.0))
            wanted = wanted - moved_over
            busy = jnp.maximum(busy_line, jnp.max(best_over, axis=0, keepdims=True))
        else:
            send_over, busy = jnp.full((line, 1), float(count), jnp.float32), busy_line
        for i, send in enumerate((send_left, send_right, send_over)):
            table_ref[3 * step + i] = send.astype(jnp.int32)
        if step <= opened:
            first = jnp.where(even, send_right, send_left)
            second = jnp.where(even, send_left, send_right)
            for i, send in enumerate((first, second, send_over)):
                name = write(3 * step + i, send)
                if i == 2 and step >= FIRST_OVER:
                    gone.append(name)
            come_left, come_right = of(send_left, me + 1), of(send_right, me - 1)
            names += [jnp.where(even, come_left, come_right), jnp.where(even, come_right, come_left)]
        left = left - anywhere(moved_left)
        right = right + anywhere(moved_right)
        length = jnp.where(jnp.where(lane == 0, busy_line, busy) > 0.0, step + 1, length)
    length_ref[...] = length

    names = names[: owned + 2 * opened]
    row = 0
    for side, queue in ((0, names), (1, names), (0, gone)):
        for n in range(owned):
            scales = [
                jnp.where(ours[side] == me * owned + n, (codes_ref[t].astype(jnp.float32) - 3.5) * 0.5, 0.0)
                for t, ours in enumerate(pairs)
            ]
            for name in queue:
                weight = jnp.zeros((1, 1), jnp.float32)
                for scale, ours in zip(scales, pairs):
                    weight = weight + jnp.where(name == ours[1 - side], scale, 0.0)
                weight_ref[row] = jnp.broadcast_to(weight, weight_ref.shape[1:])
                row += 1


def plan_rounds(me, term_nodes, weight_codes, line, owned, rounds, opened, cols):
    overs = opened + 1 - FIRST_OVER
    rows = owned * (2 * (owned + 2 * opened) + overs)
    slots, weights, tables, lengths = pl.pallas_call(
        functools.partial(plan_kernel, line, owned, term_nodes.shape[0], rounds, opened),
        out_shape=[
            jax.ShapeDtypeStruct((3 * (opened + 1), 1, cols), jnp.int32),
            jax.ShapeDtypeStruct((rows, 1, cols), jnp.float32),
            jax.ShapeDtypeStruct((3 * rounds, line, 1), jnp.int32),
            jax.ShapeDtypeStruct((line, 2), jnp.int32),
        ],
        in_specs=[pl.BlockSpec(memory_space=pltpu.SMEM)] * 3,
        out_specs=[pl.BlockSpec(memory_space=pltpu.VMEM)] * 4,
        cost_estimate=pl.CostEstimate(flops=1000, bytes_accessed=1000, transcendentals=0),
    )(me, term_nodes, weight_codes)
    return slots, weights, tables.reshape(rounds, 3, line), lengths[0]


def split(value):
    high = value.astype(jnp.bfloat16)
    return high, (value - high.astype(jnp.float32)).astype(jnp.bfloat16)


def dot3(left, right):
    dot = functools.partial(jnp.dot, preferred_element_type=jnp.float32)
    return dot(left[0], right[0]) + (dot(left[0], right[1]) + dot(left[1], right[0]))


def product(left, right):
    return (
        dot3(left[0], right[0]) - dot3(left[1], right[1]),
        dot3(left[0], right[1]) + dot3(left[1], right[0]),
    )


def pair(high_ref, low_ref, n):
    return [(high_ref[n, c], low_ref[n, c]) for c in range(2)]


def put(high_ref, low_ref, n, c, rows, cols, value):
    high, low = split(value)
    high_ref[n, c, rows, cols] = high
    low_ref[n, c, rows, cols] = low


def block(index, size):
    return pl.ds(pl.multiple_of(index * size, size), size)


def choose_kernel(rows, owned, copies, slot_ref, *refs):
    outs = refs[len(refs) - len(rows) - copies :]
    own, arrived = refs[0], refs[1 : len(refs) - len(rows) - copies]
    for row, out_ref in zip(rows, outs):
        slot = jnp.broadcast_to(slot_ref[row], out_ref.shape[1:])
        for c in range(2):
            value = own[c, 0]
            for m in range(1, owned):
                value = jnp.where(slot == m, own[c, m], value)
            for k, node in enumerate(arrived):
                value = jnp.where(slot == owned + k, node[c], value)
            out_ref[c] = value
    for m in range(copies):
        for c in range(2):
            outs[len(rows) + m][c] = own[c, m]


def early_kernel(subs, reps, names, where_ref, weight_ref, *refs):
    outs = 2 + subs - 1 + 4
    refs, (u_ref, v_ref, *rest) = refs[: len(refs) - outs], refs[len(refs) - outs :]
    x_refs, (row_high, row_low, col_high, col_low) = rest[: subs - 1], rest[subs - 1 :]
    own, beside, refs = refs[0], refs[1:reps], refs[reps:]
    rows, cols = own.shape[2:]
    owned = own.shape[1]
    across = [refs[m * (subs - 1) : (m + 1) * (subs - 1)] for m in range(owned)]
    arrived = refs[owned * (subs - 1) :]
    every = slice(None)
    for n in range(owned):
        for c in range(2):
            for i in range(reps):
                at = block(where_ref[subs + i], cols)
                put(row_high, row_low, n, c, every, at, (own if i == 0 else beside[i - 1])[c, n])
            for i in range(subs):
                matrix = own[c, n] if i == 0 else across[n][i - 1][c]
                put(col_high, col_low, n, c, block(where_ref[i], rows), every, matrix)
            nodes = [own[c, m] for m in range(owned)] + [a[c] for a in arrived]
            u_ref[n, c] = sum(weight_ref[n * names + k] * node for k, node in enumerate(nodes))
            v_ref[n, c] = sum(weight_ref[(owned + n) * names + k] * node for k, node in enumerate(nodes))
            for j in range(subs - 1):
                x_refs[j][n, c] = sum(weight_ref[n * names + m] * across[m][j][c] for m in range(owned))


def mix_kernel(subs, names, seen, arrived, gone, weight_ref, u_ref, v_ref, *refs):
    x_refs, items, refs = refs[: subs - 1], refs[subs - 1 : subs - 1 + arrived], refs[subs - 1 + arrived :]
    over, (u_out, v_out, *x_outs) = refs[: len(refs) - subs - 1], refs[len(refs) - subs - 1 :]
    owned = u_ref.shape[0]
    for n in range(owned):
        for c in range(2):
            u, v = u_ref[n, c], v_ref[n, c]
            for k, item in enumerate(items):
                u = u + weight_ref[n * names + seen + k] * item[c]
                v = v + weight_ref[(owned + n) * names + seen + k] * item[c]
            u_out[n, c], v_out[n, c] = u, v
            for j in range(subs - 1):
                x = x_refs[j][n, c]
                for k in range(len(over) // (subs - 1)):
                    x = x + weight_ref[2 * owned * names + n * gone + k] * over[k * (subs - 1) + j][c]
                x_outs[j][n, c] = x


def sum_kernel(subs, reps, where_ref, row_high, row_low, col_high, col_low, *refs):
    u, v, (out_ref, v_high, v_low, u_high, u_low) = refs[:subs], refs[subs : subs + reps], refs[subs + reps :]
    rows, cols = out_ref.shape[2:]
    for n in range(out_ref.shape[0]):
        for c in range(2):
            for i in range(subs):
                put(u_high, u_low, n, c, block(where_ref[i], rows), slice(None), u[i][n, c])
            for i in range(reps):
                put(v_high, v_low, n, c, slice(None), block(where_ref[subs + i], cols), v[i][n, c])
        one = product(pair(row_high, row_low, n), pair(u_high, u_low, n))
        two = product(pair(v_high, v_low, n), pair(col_high, col_low, n))
        out_ref[n, 0] = one[0] + two[0]
        out_ref[n, 1] = one[1] + two[1]


def late_kernel(subs, first, stride, where_ref, weight_ref, sum_ref, row_high, row_low, *refs):
    over, out_ref = refs[: subs - 1], refs[subs - 1]
    rows = sum_ref.shape[2]
    depth = row_high.shape[3] // subs
    for n in range(sum_ref.shape[0]):
        real, imag = sum_ref[n, 0], sum_ref[n, 1]
        for j in range(subs - 1):
            at = block(where_ref[1 + j], depth)
            left = [(row_high[n, c, :, at], row_low[n, c, :, at]) for c in range(2)]
            one = product(left, [split(weight_ref[first + stride * n] * over[j][c]) for c in range(2)])
            real, imag = real + one[0], imag + one[1]
        out_ref[n, 0] = real
        out_ref[n, 1] = imag


def last_kernel(reps, cells, where_ref, pick_ref, col_high, col_low, *refs):
    s, (out_ref, s_high, s_low) = refs[:reps], refs[reps:]
    cols = out_ref.shape[3]
    for n in range(out_ref.shape[1]):
        for c in range(2):
            for i in range(reps):
                put(s_high, s_low, n, c, slice(None), block(where_ref[cells + i], cols), s[i][n, c])
        real, imag = product(pair(s_high, s_low, n), pair(col_high, col_low, pick_ref[n]))
        out_ref[0, n] = real
        out_ref[1, n] = imag


def call(kernel, scalars, arrays, outs, scratch=()):
    return pl.pallas_call(
        kernel,
        out_shape=outs,
        in_specs=[pl.BlockSpec(memory_space=pltpu.SMEM)] * len(scalars)
        + [pl.BlockSpec(memory_space=pltpu.VMEM)] * len(arrays),
        out_specs=jax.tree.map(lambda _: pl.BlockSpec(memory_space=pltpu.VMEM), outs),
        scratch_shapes=list(scratch),
        compiler_params=pltpu.CompilerParams(vmem_limit_bytes=VMEM_BYTES),
        cost_estimate=pl.CostEstimate(flops=1000, bytes_accessed=1000, transcendentals=0),
    )(*scalars, *arrays)


def shifts(array, axis):
    size = lax.axis_size(axis)
    return [lax.ppermute(array, axis, [(i, (i + j) % size) for i in range(size)]) for j in range(1, size)]


def places(axis):
    size = lax.axis_size(axis)
    return [(lax.axis_index(axis) - j) % size for j in range(size)]


def body(meson_nodes, term_nodes, weight_codes, resident_pick):
    line = lax.axis_size("node")
    subs, reps = lax.axis_size("sub"), lax.axis_size("rep")
    _, owned, rows, cols = meson_nodes.shape
    count = owned * line
    terms = term_nodes.shape[0]
    me = lax.axis_index("node")
    base = me * owned
    to_left = [(z + 1, z) for z in range(line - 1)]
    to_right = [(z, z + 1) for z in range(line - 1)]
    node_shape = (2, rows, cols)
    nodes_shape = (owned, 2, rows, cols)
    depth = rows * subs
    fixed = min(line - 1, UNROLLED)
    opened = fixed + 1

    def out(shape, dtype=jnp.float32):
        return jax.ShapeDtypeStruct(shape, dtype)

    slots, weights, tables, length = plan_rounds(
        me.reshape(1), term_nodes, weight_codes, line, owned, round_bound(line, owned, terms), opened, cols
    )

    names = owned + 2 * opened
    gone = opened + 1 - FIRST_OVER
    pairs = [[(z, z + 1) for z in range(start, line - 1, 2)] for start in range(2)]
    swaps = [pair + [(j, i) for i, j in pair] for pair in pairs]

    def choose(step, kinds, came, copies=0):
        return call(
            functools.partial(choose_kernel, [3 * step + kind for kind in kinds], owned, copies),
            [],
            [slots, meson_nodes, *came],
            [out(node_shape)] * (len(kinds) + copies),
        )

    def meet(first, second):
        return [lax.ppermute(item, "node", swap) for item, swap in zip((first, second), swaps)]

    own = None
    came, across, over = [], [], []
    for step in range(fixed):
        if step == 0:
            first, second, *own = choose(step, (0, 1), came, owned)
        elif step < FIRST_OVER:
            first, second = choose(step, (0, 1), came)
        else:
            first, second, *own = choose(step, (0, 1, 2), came)
        last = owned if step == FIRST_OVER - 1 else step + 1
        beyond = [x for item in (own[step:last] if step < FIRST_OVER else own) for x in shifts(item, "sub")]
        new, beyond = lax.optimization_barrier((meet(first, second), beyond))
        came = came + new
        if step < FIRST_OVER:
            across = across + beyond
        else:
            over = over + beyond
        if step == FIRST_OVER - 1:
            beside = shifts(meson_nodes, "rep")
            for other in shifts(length, "grp"):
                length = jnp.maximum(length, other)
            came, beside, length = lax.optimization_barrier((came, beside, length))
            before = len(came)

    where = jnp.stack([*places("sub"), *places("rep")]).astype(jnp.int32)
    picks = lax.dynamic_slice_in_dim(resident_pick, base, owned)

    row_part, col_part = (owned, 2, rows, depth), (owned, 2, depth, cols)
    *early, row_high, row_low, col_high, col_low = call(
        functools.partial(early_kernel, subs, reps, names),
        [where],
        [weights, meson_nodes, *beside, *across, *came[:before]],
        [out(nodes_shape)] * (subs + 1) + [out(row_part, jnp.bfloat16)] * 2 + [out(col_part, jnp.bfloat16)] * 2,
    )

    def mixed(came, over):
        return call(
            functools.partial(mix_kernel, subs, names, owned + before, len(came) - before, gone),
            [],
            [weights, *early, *came[before:], *over],
            [out(nodes_shape)] * (subs + 1),
        )

    def sums(u, v):
        scratch = [pltpu.VMEM(row_part, jnp.bfloat16)] * 2 + [pltpu.VMEM(col_part, jnp.bfloat16)] * 2
        return call(
            functools.partial(sum_kernel, subs, reps),
            [where],
            [row_high, row_low, col_high, col_low, *u, v, *shifts(v, "rep")],
            out(nodes_shape),
            scratch,
        )

    def finish(summed):
        scratch = [pltpu.VMEM(row_part, jnp.bfloat16)] * 2
        return call(
            functools.partial(last_kernel, reps, subs),
            [where, picks],
            [col_high, col_low, summed, *shifts(summed, "rep")],
            out(meson_nodes.shape),
            scratch,
        )

    def end(step, came, over):
        [item] = choose(step, (2,), came)
        late = shifts(item, "sub")
        item, came, over = lax.optimization_barrier((item, came, over))
        u, v, *ux = mixed(came, over)
        first = 2 * owned * names + step - FIRST_OVER
        summed = call(
            functools.partial(late_kernel, subs, first, gone),
            [where],
            [weights, sums([u, *ux], v), row_high, row_low, *late],
            out(nodes_shape),
        )
        return finish(summed)

    def short(_):
        return end(fixed, came, over)

    def middle(_):
        first, second, item = choose(fixed, (0, 1, 2), came)
        new, beyond = lax.optimization_barrier((meet(first, second), shifts(item, "sub")))
        return end(fixed + 1, came + new, over + beyond)

    def long(_):
        edges = jnp.pad(tables, ((0, 0), (0, 0), (1, 1)), constant_values=count)
        mine = lax.dynamic_slice_in_dim(edges, me, 3, axis=2)
        leading, trailing = term_nodes[:, 0], term_nodes[:, 1]
        factors = (weight_codes.astype(jnp.float32) - 3.5) * 0.5
        mine_ids = base + jnp.arange(owned, dtype=jnp.int32)
        first_mine = factors[:, None] * (leading[:, None] == mine_ids)
        second_mine = factors[:, None] * (trailing[:, None] == mine_ids)
        is_even = me % 2 == 0
        from_right, from_left = [mine[step, 0, 2] for step in range(fixed)], [mine[step, 1, 0] for step in range(fixed)]
        arrivals = []
        for right, left in zip(from_right, from_left):
            arrivals += [jnp.where(is_even, right, left), jnp.where(is_even, left, right)]
        held = jnp.zeros((count + 1, 2, rows, cols), jnp.float32)
        held = lax.dynamic_update_slice(held, jnp.swapaxes(meson_nodes, 0, 1), (base, 0, 0, 0))
        for name, array in zip(arrivals, came):
            held = lax.dynamic_update_slice_in_dim(held, array[None], name, 0)

        def add(total, mine_terms, others, name, item):
            scale = jnp.sum(mine_terms * (others == name)[:, None], axis=0)
            return total + scale[:, None, None, None] * item[None]

        def take(name):
            return lax.dynamic_index_in_dim(held, name, 0, keepdims=False)

        u = [jnp.zeros(nodes_shape, jnp.float32)] * subs
        v = jnp.zeros(nodes_shape, jnp.float32)
        for m in range(owned):
            beyond = across[m * (subs - 1) : (m + 1) * (subs - 1)]
            u = [add(total, first_mine, trailing, base + m, x) for total, x in zip(u, (meson_nodes[:, m], *beyond))]
            v = add(v, second_mine, leading, base + m, meson_nodes[:, m])
        for name, array in zip(arrivals, came):
            v = add(v, second_mine, leading, name, array)
        for step in range(FIRST_OVER, fixed):
            name = mine[step, 2, 1]
            there = over[(step - FIRST_OVER) * (subs - 1) :][: subs - 1]
            u = [add(total, first_mine, trailing, name, x) for total, x in zip(u, (take(name), *there))]

        def more(state):
            return state[0] < length[1]

        def again(state):
            step, held, u, v = state
            ids = lax.dynamic_index_in_dim(mine, step, 0, keepdims=False)
            left, right, item = lax.optimization_barrier(
                tuple(lax.dynamic_index_in_dim(held, ids[i, 1], 0, keepdims=False) for i in range(3))
            )
            from_right = lax.ppermute(left, "node", to_left)
            from_left = lax.ppermute(right, "node", to_right)
            items = [item, *shifts(item, "sub")]
            from_right, from_left = lax.optimization_barrier((from_right, from_left))
            u = [add(total, first_mine, trailing, ids[2, 1], x) for total, x in zip(u, items)]
            v = add(v, second_mine, leading, ids[0, 2], from_right)
            v = add(v, second_mine, leading, ids[1, 0], from_left)
            held = lax.dynamic_update_slice_in_dim(held, from_right[None], ids[0, 2], 0)
            held = lax.dynamic_update_slice_in_dim(held, from_left[None], ids[1, 0], 0)
            return step + 1, held, u, v

        _, _, u, v = lax.while_loop(more, again, (jnp.int32(fixed), held, u, v))
        return finish(sums(u, v))

    way = jnp.maximum(length[0] - fixed, length[1] - fixed - 1)
    return lax.switch(jnp.clip(way, 0, 2), [short, middle, long], None)


def solution(mesh):
    in_specs = (P(None, ("grp", "node"), "sub", "rep"), P("grp", None), P("grp"), P("grp"))
    out_specs = P(None, ("grp", "node"), "sub", "rep")
    return jax.shard_map(body, mesh=mesh, in_specs=in_specs, out_specs=out_specs, check_vma=False)
```

time: 118 us -> 84.3 us (0.71)
  between operations: 24.3 us -> 1.41 us
  local copies, waits for them, and re-layouts: 17.1 us -> 3.75 us
  Pallas kernels: 17.2 us -> 28.3 us
  other arithmetic: 9.05 us -> 0.76 us
  waiting for transfers between devices: 19.8 us -> 27.7 us
  loops' own time: 6.06 us -> 0.27 us
  starting transfers between devices: 23.8 us -> 21.7 us
    pallas_call x4 -> x9, Pallas kernels: 14.9 us -> 26 us  [call(): pl.pallas_call(kernel, out_shape=outs, in_specs=[pl.BlockSpec(memory_spac...]
    ppermute x7 -> x8, waiting for transfers between devices: 10.5 us -> 16.8 us  [shifts(): lax.ppermute(array, axis, [(i, (i + j) % size) for i in range(size)])]
    cond x16 -> x0, local copies, waits for them, and re-layouts: 5.83 us -> none
    another operation x1, loops' own time: 6.06 us -> 0.27 us  [body(): return lax.switch(jnp.clip(way, 0, 2), [short, middle, long], None)]
    select_n x5 -> x0, other arithmetic: 5.25 us -> none  [choose(): value = jnp.where(index == name, array, value)]
    another operation x4 -> x0, local copies, waits for them, and re-layouts: 4.05 us -> none  [the longest x1 3.85 us: body(): names = jnp.stack(own_names + [name for name, _ in came])]
    ppermute x6, starting transfers between devices: 18.1 us -> 14.9 us  [meet(): lax.ppermute(item, 'node', swap)]
    slice x4 -> x1, local copies, waits for them, and re-layouts: 3.33 us -> 0.66 us  [body(): way = jnp.maximum(length[0] - fixed, length[1] - fixed - 1)]
  transfers between devices with their start and end apart: 13 -> 14, of which waited for: 7 -> 8; matrix products, arithmetic and copies ran while one was open for 16% -> 3% of each run, Pallas kernels for 8% -> 15%
where the time goes in v2:
time: 84.3 us; the launch traced here: 83.8 us
  Pallas kernels  28.3 us (34%)
  waiting for transfers between devices  27.7 us (33%)
  starting transfers between devices  21.7 us (26%)
  local copies, waits for them, and re-layouts  3.75 us (4%)
  between operations  1.41 us (2%)
    pallas_call x9, Pallas kernels, call(): pl.pallas_call(kernel, out_shape=outs, in_specs=[pl.BlockSpec(memory_spac...  26 us
    ppermute x8, waiting for transfers between devices, shifts(): lax.ppermute(array, axis, [(i, (i + j) % size) for i in range(size)])  16.8 us
    ppermute x6, starting transfers between devices, meet(): lax.ppermute(item, 'node', swap)  14.9 us
    ppermute x6, waiting for transfers between devices, meet(): lax.ppermute(item, 'node', swap)  10.8 us
    ppermute x8, starting transfers between devices, shifts(): lax.ppermute(array, axis, [(i, (i + j) % size) for i in range(size)])  6.74 us
    unnamed x11, local copies, waits for them, and re-layouts  2.33 us
    pallas_call x1, Pallas kernels, plan_rounds(): pl.pallas_call(functools.partial(plan_kernel, line, owned, term_nodes.sha...  2.29 us
  transfers between devices with their start and end apart: 14, of which 8 were waited for; matrix products, arithmetic and copies ran while one was open for 3% of the time, Pallas kernels for 15%

profile of v2, /device:TPU:0, one launch (start us, length us, event | category | flops | bytes accessed | tf_op | source)
XLA Modules:
  0.0 83.8 jit_solution(13155977301519779071)
XLA Ops:
  1.4 2.3 %shard_map.49 = (s32[15,1,256]{2,1,0:T(1,128)S(1)}, f32[46,1,256]{2,1,0:T(1,128)S(1)}, s32[27,4,1]{2,1,0:T(4,128)S(1)}, s32[4,2]{1,0:T(4,128)}) custom-call(s32[1]{0:T(128)} %bitcast.30.me_ref, s32[4,2]{1,0:T(4,128)} %copy.17.terms_ref, s32[4]{0:T(128)} %codes_ref.1), custom_call_target="tpu_custom_call" | custom-call | flops 1000 | bytes 1000 | tf_op jit(solution)/shard_map/pallas_call | solution.py:115
  5.0 3.1 %collective-permute-start.14 = (f32[2,256,256]{2,1,0:T(8,128)S(1)}, f32[2,256,256]{2,1,0:T(8,128)S(1)}, u32[]{:S(2)}, u32[]{:S(2)}) collective-permute-start(f32[2,256,256]{2,1,0:T(8,128)S(1)} %get-tuple-element.312), channel_id=1, source_target_pairs={{0,4},{8,12},{4,0},{12,8},{1,5},{9,13},{5,1},{13,9},{2,6},{10,14},... | collective-permute-start | bytes 1572872 | tf_op jit(solution)/shard_map/ppermute | solution.py:323
  9.6 1.5 %collective-permute-start.16 = (f32[2,256,256]{2,1,0:T(8,128)S(1)}, f32[2,256,256]{2,1,0:T(8,128)}, u32[]{:S(2)}, u32[]{:S(2)}) collective-permute-start(f32[2,256,256]{2,1,0:T(8,128)S(1)} %get-tuple-element.314), channel_id=1, source_target_pairs={{0,2},{2,0},{1,3},{3,1},{4,6},{6,4},{5,7},{7,5},{8,10},{10,8},{9,1... | collective-permute-start | bytes 1572872 | tf_op jit(solution)/shard_map/ppermute | solution.py:278
  11.6 8.4 %collective-permute-done.14.refs_1_.refs_4_ = f32[2,256,256]{2,1,0:T(8,128)S(1)} collective-permute-done((f32[2,256,256]{2,1,0:T(8,128)S(1)}, f32[2,256,256]{2,1,0:T(8,128)S(1)}, u32[]{:S(2)}, u32[]{:S(2)}) %collective-permute-start.14) | collective-permute-done | bytes 524320 | tf_op jit(solution)/shard_map/ppermute | solution.py:323
  20.0 4.5 %collective-permute-done.16.refs_2_ = f32[2,256,256]{2,1,0:T(8,128)} collective-permute-done((f32[2,256,256]{2,1,0:T(8,128)S(1)}, f32[2,256,256]{2,1,0:T(8,128)}, u32[]{:S(2)}, u32[]{:S(2)}) %collective-permute-start.16) | collective-permute-done | bytes 524320 | tf_op jit(solution)/shard_map/ppermute | solution.py:278
  24.6 1.5 %shard_map.51 = (f32[2,256,256]{2,1,0:T(8,128)S(1)}, f32[2,256,256]{2,1,0:T(8,128)S(1)}) custom-call(s32[15,1,256]{2,1,0:T(1,128)S(1)} %get-tuple-element.311.slot_ref, f32[2,2,256,256]{3,2,1,0:T(8,128)} %refs_0_.7, f32[2,256,256]{2,1,0:T(8,128)S(1)} %collective-permute-done.14.refs_1_.refs_4_, f32[2,256,256]{2,1,0:T(8,128)} %collective-permute-done.15.refs_2_.refs_5_), custom_call_target="tpu_custom_call" | custom-call | flops 1000 | bytes 1000 | tf_op jit(solution)/shard_map/pallas_call | solution.py:264
  26.1 3.7 %collective-permute-start.17 = (f32[2,256,256]{2,1,0:T(8,128)S(1)}, f32[2,256,256]{2,1,0:T(8,128)}, u32[]{:S(2)}, u32[]{:S(2)}) collective-permute-start(f32[2,256,256]{2,1,0:T(8,128)S(1)} %get-tuple-element.317), channel_id=1, source_target_pairs={{0,4},{8,12},{4,0},{12,8},{1,5},{9,13},{5,1},{13,9},{2,6},{10,14},... | collective-permute-start | bytes 1572872 | tf_op jit(solution)/shard_map/ppermute | solution.py:323
  32.0 1.5 %collective-permute-start.21 = (s32[2]{0:T(128)S(1)}, s32[2]{0:T(128)S(1)}, u32[]{:S(2)}, u32[]{:S(2)}) collective-permute-start(s32[2]{0:T(128)S(1)} %slice_bitcast_fusion.4), channel_id=1, source_target_pairs={{0,16},{16,0},{1,17},{17,1},{2,18},{18,2},{3,19},{19,3},{4,20},{20... | collective-permute-start | bytes 32 | tf_op jit(solution)/shard_map/ppermute | solution.py:278
  33.5 2.0 %collective-permute-done.21 = s32[2]{0:T(128)S(1)} collective-permute-done((s32[2]{0:T(128)S(1)}, s32[2]{0:T(128)S(1)}, u32[]{:S(2)}, u32[]{:S(2)}) %collective-permute-start.21) | collective-permute-done | bytes 40 | tf_op jit(solution)/shard_map/ppermute | solution.py:278
  36.2 2.4 %collective-permute-done.17.refs_3_.refs_6_ = f32[2,256,256]{2,1,0:T(8,128)} collective-permute-done((f32[2,256,256]{2,1,0:T(8,128)S(1)}, f32[2,256,256]{2,1,0:T(8,128)}, u32[]{:S(2)}, u32[]{:S(2)}) %collective-permute-start.17) | collective-permute-done | bytes 524320 | tf_op jit(solution)/shard_map/ppermute | solution.py:323
  38.6 2.1 %shard_map.52 = (f32[2,256,256]{2,1,0:T(8,128)S(1)}, f32[2,256,256]{2,1,0:T(8,128)S(1)}, f32[2,256,256]{2,1,0:T(8,128)S(1)}) custom-call(s32[15,1,256]{2,1,0:T(1,128)S(1)} %get-tuple-element.311.slot_ref, f32[2,2,256,256]{3,2,1,0:T(8,128)} %refs_0_.7, f32[2,256,256]{2,1,0:T(8,128)S(1)} %collective-permute-done.14.refs_1_.refs_4_, ...), custom_call_target="tpu_custom_call" | custom-call | flops 1000 | bytes 1000 | tf_op jit(solution)/shard_map/pallas_call | solution.py:264
  40.7 3.7 %collective-permute-start.22 = (f32[2,256,256]{2,1,0:T(8,128)S(1)}, f32[2,256,256]{2,1,0:T(8,128)}, u32[]{:S(2)}, u32[]{:S(2)}) collective-permute-start(f32[2,256,256]{2,1,0:T(8,128)S(1)} %get-tuple-element.328), channel_id=1, source_target_pairs={{0,4},{8,12},{4,0},{12,8},{1,5},{9,13},{5,1},{13,9},{2,6},{10,14},... | collective-permute-start | bytes 1572872 | tf_op jit(solution)/shard_map/ppermute | solution.py:323
  44.4 1.5 %collective-permute-start.23 = (f32[2,256,256]{2,1,0:T(8,128)S(1)}, f32[2,256,256]{2,1,0:T(8,128)}, u32[]{:S(2)}, u32[]{:S(2)}) collective-permute-start(f32[2,256,256]{2,1,0:T(8,128)S(1)} %get-tuple-element.329), channel_id=1, source_target_pairs={{4,8},{8,4},{5,9},{9,5},{6,10},{10,6},{7,11},{11,7},{20,24},{24,20... | collective-permute-start | bytes 1572872 | tf_op jit(solution)/shard_map/ppermute | solution.py:323
  45.9 1.5 %collective-permute-start.24 = (f32[2,256,256]{2,1,0:T(8,128)S(1)}, f32[2,256,256]{2,1,0:T(8,128)}, u32[]{:S(2)}, u32[]{:S(2)}) collective-permute-start(f32[2,256,256]{2,1,0:T(8,128)S(1)} %get-tuple-element.330), channel_id=1, source_target_pairs={{0,2},{2,0},{1,3},{3,1},{4,6},{6,4},{5,7},{7,5},{8,10},{10,8},{9,1... | collective-permute-start | bytes 1572872 | tf_op jit(solution)/shard_map/ppermute | solution.py:278
  47.6 4.5 %shard_map.53 = (f32[2,2,256,256]{3,2,1,0:T(8,128)S(1)}, f32[2,2,256,256]{3,2,1,0:T(8,128)S(1)}, f32[2,2,256,256]{3,2,1,0:T(8,128)S(1)}, bf16[2,2,256,512]{3,2,1...) custom-call(s32[4]{0:T(128)S(1)} %pad_add_fusion.where_ref, ...), custom_call_target="tpu_custom_call" | custom-call | flops 1000 | bytes 1000 | tf_op jit(solution)/shard_map/pallas_call | solution.py:264
  55.3 27.6 %conditional.1 = (f32[2,2,256,256]{3,2,1,0:T(8,128)S(1)}) conditional(s32[]{:T(128)} %bitcast.32, (s32[15,1,256]{2,1,0:T(1,128)S(1)}, f32[2,2,256,256]{3,2,1,0:T(8,128)}, f32[2,256,256]{2,1,0:T(8,128)S(1)}, f32[2,256,256]{2,1,0:T(8,128)}, f32[2,256,256]{2,1,0:T(8,128)}, /*index=5*/f32[2,256,256]{2,1,0:T(8,128)}, ...), branch_computations={%region_0.1_spmd, %region_1.2_spmd, %region_2.19_spmd} | conditional | flops 8653207 | bytes 92810688 | solution.py:472
  55.3 2.2 %branch_0_fun.5 = f32[2,256,256]{2,1,0:T(8,128)S(1)} custom-call(s32[15,1,256]{2,1,0:T(1,128)S(1)} %get-tuple-element.184.slot_ref, f32[2,2,256,256]{3,2,1,0:T(8,128)} %get-tuple-element.185.refs_0_, f32[2,256,256]{2,1,0:T(8,128)S(1)} %get-tuple-element.186.refs_1_, f32[2,256,256]{2,1,0:T(8,128)} %get-tuple-element.187.refs_2_, ...), custom_call_target="tpu_custom_call" | custom-call | flops 1000 | bytes 1000 | tf_op jit(solution)/shard_map/cond/branch_0_fun/pallas_call | solution.py:264
  57.4 1.8 %branch_0_fun.6 = (f32[2,2,256,256]{3,2,1,0:T(8,128)S(1)}, f32[2,2,256,256]{3,2,1,0:T(8,128)S(1)}, f32[2,2,256,256]{3,2,1,0:T(8,128)S(1)}) custom-call(f32[46,1,256]{2,1,0:T(1,128)S(1)} %get-tuple-element.178.weight_ref, f32[2,2,256,256]{3,2,1,0:T(8,128)S(1)} %get-tuple-element.181.u_ref, f32[2,2,256,256]{3,2,1,0:T(8,128)S(1)} %get-tuple-element.182.v_ref, ...), custom_call_target="tpu_custom_call" | custom-call | flops 1000 | bytes 1000 | tf_op jit(solution)/shard_map/cond/branch_0_fun/pallas_call | solution.py:264
  59.3 1.6 %collective-permute-start.1 = (f32[2,256,256]{2,1,0:T(8,128)S(1)}, f32[2,256,256]{2,1,0:T(8,128)S(1)}, u32[]{:S(2)}, u32[]{:S(2)}) collective-permute-start(f32[2,256,256]{2,1,0:T(8,128)S(1)} %branch_0_fun.5), channel_id=1, source_target_pairs={{0,2},{2,0},{1,3},{3,1},{4,6},{6,4},{5,7},{7,5},{8,10},{10,8},{9,1... | collective-permute-start | bytes 1572872 | tf_op jit(solution)/shard_map/cond/branch_0_fun/ppermute | solution.py:278
  61.9 6.3 %branch_0_fun.7.sum_ref = f32[2,2,256,256]{3,2,1,0:T(8,128)S(1)} custom-call(s32[4]{0:T(128)S(1)} %get-tuple-element.174.where_ref, bf16[2,2,256,512]{3,2,1,0:T(8,128)(2,1)} %get-tuple-element.179.row_high, bf16[2,2,256,512]{3,2,1,0:T(8,128)(2,1)} %get-tuple-element.180.row_low, bf16[2,2,512,256]{3,2,1,0:T(8,128)(2,1)} %get-tuple-element.176.col_high, ...), custom_call_target="tpu_custom_call" | custom-call | flops 1000 | bytes 1000 | tf_op jit(solution)/shard_map/cond/branch_0_fun/pallas_call | solution.py:264
  68.2 5.4 %collective-permute-done.1.refs_0_ = f32[2,256,256]{2,1,0:T(8,128)S(1)} collective-permute-done((f32[2,256,256]{2,1,0:T(8,128)S(1)}, f32[2,256,256]{2,1,0:T(8,128)S(1)}, u32[]{:S(2)}, u32[]{:S(2)}) %collective-permute-start.1) | collective-permute-done | bytes 524320 | tf_op jit(solution)/shard_map/cond/branch_0_fun/ppermute | solution.py:278
  73.6 2.6 %branch_0_fun.8.refs_0_ = f32[2,2,256,256]{3,2,1,0:T(8,128)S(1)} custom-call(s32[4]{0:T(128)S(1)} %get-tuple-element.174.where_ref, f32[46,1,256]{2,1,0:T(1,128)S(1)} %get-tuple-element.178.weight_ref, f32[2,2,256,256]{3,2,1,0:T(8,128)S(1)} %branch_0_fun.7.sum_ref, bf16[2,2,256,512]{3,2,1,0:T(8,128)(2,1)} %get-tuple-element.179.row_high, ...), custom_call_target="tpu_custom_call" | custom-call | flops 1000 | bytes 1000 | tf_op jit(solution)/shard_map/cond/branch_0_fun/pallas_call | solution.py:264
  76.3 2.6 %collective-permute-done.2.refs_1_ = f32[2,2,256,256]{3,2,1,0:T(8,128)S(1)} collective-permute-done((f32[2,2,256,256]{3,2,1,0:T(8,128)S(1)}, f32[2,2,256,256]{3,2,1,0:T(8,128)S(1)}, u32[]{:S(2)}, u32[]{:S(2)}) %collective-permute-start.2) | collective-permute-done | bytes 1048608 | tf_op jit(solution)/shard_map/cond/branch_0_fun/ppermute | solution.py:278
  78.9 3.7 %branch_0_fun.9 = f32[2,2,256,256]{3,2,1,0:T(8,128)S(1)} custom-call(s32[4]{0:T(128)S(1)} %get-tuple-element.174.where_ref, s32[2]{0:T(128)S(1)} %get-tuple-element.175.pick_ref, bf16[2,2,512,256]{3,2,1,0:T(8,128)(2,1)} %get-tuple-element.176.col_high, bf16[2,2,512,256]{3,2,1,0:T(8,128)(2,1)} %get-tuple-element.177.col_low, ...), custom_call_target="tpu_custom_call" | custom-call | flops 1000 | bytes 1000 | tf_op jit(solution)/shard_map/cond/branch_0_fun/pallas_call | solution.py:264
  (31 shorter events, 11.7 us)
Async XLA Ops:
  0.0 47.4 %copy-start.11 = (s32[8]{0:T(128)S(1)}, s32[8]{0:T(128)}, u32[]{:S(2)}) copy-start(s32[8]{0:T(128)} %param.12) | copy-start | bytes 100
  5.0 15.0 %collective-permute-start.14 = (f32[2,256,256]{2,1,0:T(8,128)S(1)}, f32[2,256,256]{2,1,0:T(8,128)S(1)}, u32[]{:S(2)}, u32[]{:S(2)}) collective-permute-start(f32[2,256,256]{2,1,0:T(8,128)S(1)} %get-tuple-element.312), channel_id=1, source_target_pairs={{0,4},{8,12},{4,0},{12,8},{1,5},{9,13},{5,1},{13,9},{2,6},{10,14},... | collective-permute-start | bytes 1572872 | tf_op jit(solution)/shard_map/ppermute | solution.py:323
  8.1 11.9 %collective-permute-start.15 = (f32[2,256,256]{2,1,0:T(8,128)S(1)}, f32[2,256,256]{2,1,0:T(8,128)}, u32[]{:S(2)}, u32[]{:S(2)}) collective-permute-start(f32[2,256,256]{2,1,0:T(8,128)S(1)} %get-tuple-element.313), channel_id=1, source_target_pairs={{4,8},{8,4},{5,9},{9,5},{6,10},{10,6},{7,11},{11,7},{20,24},{24,20... | collective-permute-start | bytes 1572872 | tf_op jit(solution)/shard_map/ppermute | solution.py:323
  9.6 15.0 %collective-permute-start.16 = (f32[2,256,256]{2,1,0:T(8,128)S(1)}, f32[2,256,256]{2,1,0:T(8,128)}, u32[]{:S(2)}, u32[]{:S(2)}) collective-permute-start(f32[2,256,256]{2,1,0:T(8,128)S(1)} %get-tuple-element.314), channel_id=1, source_target_pairs={{0,2},{2,0},{1,3},{3,1},{4,6},{6,4},{5,7},{7,5},{8,10},{10,8},{9,1... | collective-permute-start | bytes 1572872 | tf_op jit(solution)/shard_map/ppermute | solution.py:278
  11.1 27.5 %collective-permute-start.20 = (f32[2,2,256,256]{3,2,1,0:T(8,128)}, f32[2,2,256,256]{3,2,1,0:T(8,128)S(1)}, u32[]{:S(2)}, u32[]{:S(2)}) collective-permute-start(f32[2,2,256,256]{3,2,1,0:T(8,128)} %refs_0_.7), channel_id=1, source_target_pairs={{0,1},{1,0},{2,3},{3,2},{4,5},{5,4},{6,7},{7,6},{8,9},{9,8},{10,11... | collective-permute-start | bytes 3145736 | tf_op jit(solution)/shard_map/ppermute | solution.py:278
  11.1 25.1 %collective-permute-start.19 = (f32[2,256,256]{2,1,0:T(8,128)S(1)}, f32[2,256,256]{2,1,0:T(8,128)S(1)}, u32[]{:S(2)}, u32[]{:S(2)}) collective-permute-start(f32[2,256,256]{2,1,0:T(8,128)S(1)} %get-tuple-element.319), channel_id=1, source_target_pairs={{0,2},{2,0},{1,3},{3,1},{4,6},{6,4},{5,7},{7,5},{8,10},{10,8},{9,1... | collective-permute-start | bytes 1572872 | tf_op jit(solution)/shard_map/ppermute | solution.py:278
  26.1 29.2 %copy-start.8 = (s32[4,2]{0,1:T(2,128)S(1)}, s32[4,2]{0,1:T(2,128)}, u32[]{:S(2)}) copy-start(s32[4,2]{0,1:T(2,128)} %param.10) | copy-start | bytes 100
  26.1 29.1 %copy-start.10 = (s32[4]{0:T(128)S(1)}, s32[4]{0:T(128)}, u32[]{:S(2)}) copy-start(s32[4]{0:T(128)} %codes_ref.1) | copy-start | bytes 52
  26.1 12.5 %collective-permute-start.17 = (f32[2,256,256]{2,1,0:T(8,128)S(1)}, f32[2,256,256]{2,1,0:T(8,128)}, u32[]{:S(2)}, u32[]{:S(2)}) collective-permute-start(f32[2,256,256]{2,1,0:T(8,128)S(1)} %get-tuple-element.317), channel_id=1, source_target_pairs={{0,4},{8,12},{4,0},{12,8},{1,5},{9,13},{5,1},{13,9},{2,6},{10,14},... | collective-permute-start | bytes 1572872 | tf_op jit(solution)/shard_map/ppermute | solution.py:323
  29.8 8.8 %collective-permute-start.18 = (f32[2,256,256]{2,1,0:T(8,128)S(1)}, f32[2,256,256]{2,1,0:T(8,128)}, u32[]{:S(2)}, u32[]{:S(2)}) collective-permute-start(f32[2,256,256]{2,1,0:T(8,128)S(1)} %get-tuple-element.318), channel_id=1, source_target_pairs={{4,8},{8,4},{5,9},{9,5},{6,10},{10,6},{7,11},{11,7},{20,24},{24,20... | collective-permute-start | bytes 1572872 | tf_op jit(solution)/shard_map/ppermute | solution.py:323
  32.0 3.5 %collective-permute-start.21 = (s32[2]{0:T(128)S(1)}, s32[2]{0:T(128)S(1)}, u32[]{:S(2)}, u32[]{:S(2)}) collective-permute-start(s32[2]{0:T(128)S(1)} %slice_bitcast_fusion.4), channel_id=1, source_target_pairs={{0,16},{16,0},{1,17},{17,1},{2,18},{18,2},{3,19},{19,3},{4,20},{20... | collective-permute-start | bytes 32 | tf_op jit(solution)/shard_map/ppermute | solution.py:278
  36.2 9.7 %copy-start.5 = (f32[2,256,256]{2,1,0:T(8,128)}, f32[2,256,256]{2,1,0:T(8,128)S(1)}, u32[]{:S(2)}) copy-start(f32[2,256,256]{2,1,0:T(8,128)S(1)} %collective-permute-done.19.refs_3_) | copy-start | bytes 1572868
  40.7 13.4 %collective-permute-start.22 = (f32[2,256,256]{2,1,0:T(8,128)S(1)}, f32[2,256,256]{2,1,0:T(8,128)}, u32[]{:S(2)}, u32[]{:S(2)}) collective-permute-start(f32[2,256,256]{2,1,0:T(8,128)S(1)} %get-tuple-element.328), channel_id=1, source_target_pairs={{0,4},{8,12},{4,0},{12,8},{1,5},{9,13},{5,1},{13,9},{2,6},{10,14},... | collective-permute-start | bytes 1572872 | tf_op jit(solution)/shard_map/ppermute | solution.py:323
  44.4 9.7 %collective-permute-start.23 = (f32[2,256,256]{2,1,0:T(8,128)S(1)}, f32[2,256,256]{2,1,0:T(8,128)}, u32[]{:S(2)}, u32[]{:S(2)}) collective-permute-start(f32[2,256,256]{2,1,0:T(8,128)S(1)} %get-tuple-element.329), channel_id=1, source_target_pairs={{4,8},{8,4},{5,9},{9,5},{6,10},{10,6},{7,11},{11,7},{20,24},{24,20... | collective-permute-start | bytes 1572872 | tf_op jit(solution)/shard_map/ppermute | solution.py:323
  45.9 9.3 %collective-permute-start.24 = (f32[2,256,256]{2,1,0:T(8,128)S(1)}, f32[2,256,256]{2,1,0:T(8,128)}, u32[]{:S(2)}, u32[]{:S(2)}) collective-permute-start(f32[2,256,256]{2,1,0:T(8,128)S(1)} %get-tuple-element.330), channel_id=1, source_target_pairs={{0,2},{2,0},{1,3},{3,1},{4,6},{6,4},{5,7},{7,5},{8,10},{10,8},{9,1... | collective-permute-start | bytes 1572872 | tf_op jit(solution)/shard_map/ppermute | solution.py:278
  59.2 2.7 %collective-permute-start = (f32[2,2,256,256]{3,2,1,0:T(8,128)S(1)}, f32[2,2,256,256]{3,2,1,0:T(8,128)S(1)}, u32[]{:S(2)}, u32[]{:S(2)}) collective-permute-start(f32[2,2,256,256]{3,2,1,0:T(8,128)S(1)} %get-tuple-element.198.refs_2_), channel_id=1, source_target_pairs={{0,1},{1,0},{2,3},{3,2},{4,5},{5,4},{6,7},{7,6},{8,9},{9,8},{10,11... | collective-permute-start | bytes 3145736 | tf_op jit(solution)/shard_map/cond/branch_0_fun/ppermute | solution.py:278
  59.3 14.3 %collective-permute-start.1 = (f32[2,256,256]{2,1,0:T(8,128)S(1)}, f32[2,256,256]{2,1,0:T(8,128)S(1)}, u32[]{:S(2)}, u32[]{:S(2)}) collective-permute-start(f32[2,256,256]{2,1,0:T(8,128)S(1)} %branch_0_fun.5), channel_id=1, source_target_pairs={{0,2},{2,0},{1,3},{3,1},{4,6},{6,4},{5,7},{7,5},{8,10},{10,8},{9,1... | collective-permute-start | bytes 1572872 | tf_op jit(solution)/shard_map/cond/branch_0_fun/ppermute | solution.py:278
  76.2 2.7 %collective-permute-start.2 = (f32[2,2,256,256]{3,2,1,0:T(8,128)S(1)}, f32[2,2,256,256]{3,2,1,0:T(8,128)S(1)}, u32[]{:S(2)}, u32[]{:S(2)}) collective-permute-start(f32[2,2,256,256]{3,2,1,0:T(8,128)S(1)} %branch_0_fun.8.refs_0_), channel_id=1, source_target_pairs={{0,1},{1,0},{2,3},{3,2},{4,5},{5,4},{6,7},{7,6},{8,9},{9,8},{10,11... | collective-permute-start | bytes 3145736 | tf_op jit(solution)/shard_map/cond/branch_0_fun/ppermute | solution.py:278
  82.9 1.0 %copy-start.7 = (f32[2,2,256,256]{3,2,1,0:T(8,128)}, f32[2,2,256,256]{3,2,1,0:T(8,128)S(1)}, u32[]{:S(2)}) copy-start(f32[2,2,256,256]{3,2,1,0:T(8,128)S(1)} %get-tuple-element.802) | copy-start | bytes 3145732
